TPU v7x, 32 devices: a whole 2x2x4 slice. The times are simulated.
32 devices in a mesh: row: 4 (over y, core), seq: 8 (over z, x).
Axes of the slice: x: 2, y: 2, z: 4, core: 2. Of those that a mesh axis runs over, the one named last changes fastest.
Arguments:
- features: bfloat16 [8, 512, 768], P('row', 'seq'), may hold values from -6 to 6
- cotangent: bfloat16 [8, 512, 768], P('row', 'seq'), may hold values from -6 to 6
- segments: int32 [8, 512], P('row'), may hold values from 0 to 3, never falling along the last dimension, each value on 1 to 256 neighbouring positions
- stem_weight: bfloat16 [6144, 768], replicated, may hold values from -0.078125 to 0.078125
- projection_weight: bfloat16 [2, 768, 2304], replicated, may hold values from -0.21875 to 0.21875
- mixing_weight: bfloat16 [2, 768, 768], replicated, may hold values from -0.875 to 0.875
- feedforward_weight: bfloat16 [2, 768, 2, 3072], replicated, may hold values from -0.21875 to 0.21875
- norm_gains: float32 [5, 768], replicated, may hold values from 0.5 to 1.5
- biases: float32 [22, 768], replicated, may hold values from -3 to 3
- stem_moment: float32 [6144, 768], P('row', 'seq'), may hold values from -192 to 192
- projection_moment: float32 [2, 768, 2304], P(None, 'seq', 'row'), may hold values from -80 to 80
- mixing_moment: float32 [2, 768, 768], P(None, 'seq', 'row'), may hold values from -40 to 40
- feedforward_moment: float32 [2, 768, 2, 3072], P(None, 'seq', None, 'row'), may hold values from -192 to 192
- gain_moment: float32 [5, 768], P(None, 'seq'), may hold values from -256 to 256
- bias_moment: float32 [22, 768], P(None, 'seq'), may hold values from -384 to 384
- stem_average: float32 [6144, 768], P('row', 'seq'), may hold values from -0.078125 to 0.078125
- projection_average: float32 [2, 768, 2304], P(None, 'seq', 'row'), may hold values from -0.21875 to 0.21875
- mixing_average: float32 [2, 768, 768], P(None, 'seq', 'row'), may hold values from -0.875 to 0.875
- feedforward_average: float32 [2, 768, 2, 3072], P(None, 'seq', None, 'row'), may hold values from -0.21875 to 0.21875
- gain_average: float32 [5, 768], P(None, 'seq'), may hold values from 0.25 to 1.75
- bias_average: float32 [22, 768], P(None, 'seq'), may hold values from -3 to 3
Outputs:
- encoded: float32 [8, 512, 768], P('row', 'seq')
- features_gradient: float32 [8, 512, 768], P('row', 'seq')
- stem_momentum: float32 [6144, 768], P('row', 'seq')
- projection_momentum: float32 [2, 768, 2304], P(None, 'seq', 'row')
- mixing_momentum: float32 [2, 768, 768], P(None, 'seq', 'row')
- feedforward_momentum: float32 [2, 768, 2, 3072], P(None, 'seq', None, 'row')
- gain_momentum: float32 [5, 768], P(None, 'seq')
- bias_momentum: float32 [22, 768], P(None, 'seq')
- stem_averaged: float32 [6144, 768], P('row', 'seq')
- projection_averaged: float32 [2, 768, 2304], P(None, 'seq', 'row')
- mixing_averaged: float32 [2, 768, 768], P(None, 'seq', 'row')
- feedforward_averaged: float32 [2, 768, 2, 3072], P(None, 'seq', None, 'row')
- gain_averaged: float32 [5, 768], P(None, 'seq')
- bias_averaged: float32 [22, 768], P(None, 'seq')
- stem_updated: float32 [6144, 768], P('row', 'seq')
- projection_updated: float32 [2, 768, 2304], P(None, 'seq', 'row')
- mixing_updated: float32 [2, 768, 768], P(None, 'seq', 'row')
- feedforward_updated: float32 [2, 768, 2, 3072], P(None, 'seq', None, 'row')
- gain_updated: float32 [5, 768], P(None, 'seq')
- bias_updated: float32 [22, 768], P(None, 'seq')
Inputs may be any that keep to these rules, and one draw needn't show every extreme that they name: `segments`: within a row the clip ids never fall; every clip spans 1 to 256 frames of one row.
All inputs are finite; a program needn't handle non-finite values.
Results may differ from a plain program's by a relative error of at most 0.02.
Values may be sent and summed in bfloat16 or wider, within the bound.
No kernel may reach another device: no remote copies, remote signals or barrier semaphores. Data moves between devices by JAX's collectives and lax.ppermute only.
A program may use at most 448 MiB of HBM per device.

v0:
```python
import math

import jax
import jax.numpy as jnp
from jax import lax
from jax.sharding import PartitionSpec as P

HEADS = 12
KERNEL = 128
GROUPS = 16


epsilon = 1e-05
masked_score = -1e30
momentum_decay = 0.9
average_decay = 0.5
rate_factors = (0.012, 0.08, 0.6, 0.03, 0.06, 0.09)
row_dims = (0, 2, 2, 3)


def extended_2(cells, sides, width):
    for axis, dim in sides:
        count = lax.axis_size(axis)
        ends = count - 1
        head = lax.slice_in_dim(cells, 0, width, axis=dim)
        tail = lax.slice_in_dim(cells, cells.shape[dim] - width, cells.shape[dim], axis=dim)
        cells = jnp.concatenate(
            [
                lax.ppermute(tail, axis, [(i, (i + 1) % count) for i in range(ends)]),
                cells,
                lax.ppermute(head, axis, [((i + 1) % count, i) for i in range(ends)]),
            ],
            axis=dim,
        )
    return cells


def layer_norm(values, gain_row, shift_row):
    centre = jnp.mean(values, axis=-1, keepdims=True)
    centred = values - centre
    spread = jnp.mean(centred * centred, axis=-1, keepdims=True)
    inverse = lax.rsqrt(spread + epsilon)
    normed = centred * inverse
    return (normed * gain_row + shift_row, normed, inverse)


def layer_norm_back(upstream, normed, inverse, gain_row):
    scaled = upstream * gain_row
    first_mean = jnp.mean(scaled, axis=-1, keepdims=True)
    second_mean = jnp.mean(scaled * normed, axis=-1, keepdims=True)
    downstream = inverse * (scaled - first_mean - normed * second_mean)
    return (downstream, jnp.sum(upstream * normed, axis=(0, 1)), jnp.sum(upstream, axis=(0, 1)))


def gelu_exact(values):
    return jax.nn.gelu(values, approximate=False)


def gelu_back(inputs, upstream):
    _, pullback = jax.vjp(gelu_exact, inputs)
    return pullback(upstream)[0]


def group_conv(extended, kernel_taps, group_count):
    return lax.conv_general_dilated(
        extended,
        kernel_taps,
        (1,),
        "VALID",
        dimension_numbers=("NWC", "WIO", "NWC"),
        feature_group_count=group_count,
        preferred_element_type=jnp.float32,
    )


def group_conv_kernel_grad(extended, upstream_low, group_count):
    return lax.conv_general_dilated(
        extended,
        upstream_low,
        (1,),
        "VALID",
        dimension_numbers=("CWN", "IWO", "WNC"),
        batch_group_count=group_count,
        preferred_element_type=jnp.float32,
    )


def flipped_taps(kernel_taps, group_count):
    tap_count, group_width, model_width = kernel_taps.shape
    split_taps = kernel_taps.reshape(tap_count, group_width, group_count, group_width)
    swapped = jnp.transpose(split_taps, (0, 3, 2, 1)).reshape(tap_count, group_width, model_width)
    return swapped[::-1]


def masked_scores(query_part, key_part, query_segments, key_segments):
    scores = jnp.einsum("rqhe,rkhe->rhqk", query_part, key_part, preferred_element_type=jnp.float32)
    allowed = query_segments[:, None, :, None] == key_segments[:, None, None, :]
    return jnp.where(allowed, scores, masked_score)


def key_slice(kv_whole, segments, start, key_block, head_count):
    row_count = kv_whole.shape[0]
    model_width = kv_whole.shape[2] // 2
    head_width = model_width // head_count
    part_rows = lax.dynamic_slice_in_dim(kv_whole, start, key_block, 1)
    part_segments = lax.dynamic_slice_in_dim(segments, start, key_block, 1)
    key_part = part_rows[:, :, :model_width].reshape(row_count, key_block, head_count, head_width)
    value_part = part_rows[:, :, model_width:].reshape(row_count, key_block, head_count, head_width)
    return (key_part, value_part, part_segments)


def attend(query_heads, kv_whole, query_segments, segments, head_count):
    row_count = query_heads.shape[0]
    tok_count = query_heads.shape[1]
    key_block = math.gcd(kv_whole.shape[1], 1024)
    block_count = kv_whole.shape[1] // key_block

    def stats_step(step_index, state):
        running_max, running_sum = state
        key_part, value_part, part_segments = key_slice(
            kv_whole, segments, step_index * key_block, key_block, head_count
        )
        scores = masked_scores(query_heads, key_part, query_segments, part_segments)
        new_max = jnp.maximum(running_max, jnp.max(scores, axis=-1))
        running_sum = running_sum * jnp.exp(running_max - new_max) + jnp.sum(
            jnp.exp(scores - new_max[..., None]), axis=-1
        )
        return (new_max, running_sum)

    start_state = (
        jnp.full((row_count, head_count, tok_count), masked_score, jnp.float32),
        jnp.zeros((row_count, head_count, tok_count), jnp.float32),
    )
    running_max, running_sum = lax.fori_loop(0, block_count, stats_step, start_state)
    log_sum = running_max + jnp.log(running_sum)

    def value_step(step_index, state):
        coarse, residue = state
        key_part, value_part, part_segments = key_slice(
            kv_whole, segments, step_index * key_block, key_block, head_count
        )
        probability = jnp.exp(
            masked_scores(query_heads, key_part, query_segments, part_segments) - log_sum[..., None]
        )
        probability_low = probability.astype(jnp.bfloat16)
        remainder_low = (probability - probability_low.astype(jnp.float32)).astype(jnp.bfloat16)
        coarse = coarse + jnp.einsum(
            "rhqk,rkhe->rqhe", probability_low, value_part, preferred_element_type=jnp.float32
        )
        residue = residue + jnp.einsum(
            "rhqk,rkhe->rqhe", remainder_low, value_part, preferred_element_type=jnp.float32
        )
        return (coarse, residue)

    zero_out = jnp.zeros(query_heads.shape, jnp.float32)
    coarse, residue = lax.fori_loop(0, block_count, value_step, (zero_out, zero_out))
    return (coarse, coarse + residue, log_sum)


def attend_back(
    query_heads, grad_heads, kv_whole, query_segments, segments, log_sum, delta, head_count
):
    row_count = query_heads.shape[0]
    frame_count = kv_whole.shape[1]
    model_width = kv_whole.shape[2] // 2
    key_block = math.gcd(frame_count, 1024)
    block_count = frame_count // key_block

    def back_step(step_index, state):
        grad_query, key_terms = state
        start = step_index * key_block
        key_part, value_part, part_segments = key_slice(
            kv_whole, segments, start, key_block, head_count
        )
        probability = jnp.exp(
            masked_scores(query_heads, key_part, query_segments, part_segments) - log_sum[..., None]
        )
        grad_prob = jnp.einsum(
            "rqhe,rkhe->rhqk", grad_heads, value_part, preferred_element_type=jnp.float32
        )
        grad_scores = (probability * (grad_prob - delta[..., None])).astype(jnp.bfloat16)
        grad_query = grad_query + jnp.einsum(
            "rhqk,rkhe->rqhe", grad_scores, key_part, preferred_element_type=jnp.float32
        )
        grad_keys = jnp.einsum(
            "rhqk,rqhe->rkhe", grad_scores, query_heads, preferred_element_type=jnp.float32
        )
        grad_values = jnp.einsum(
            "rhqk,rqhe->rkhe",
            probability.astype(jnp.bfloat16),
            grad_heads,
            preferred_element_type=jnp.float32,
        )
        both_terms = jnp.concatenate(
            [
                grad_keys.reshape(row_count, key_block, model_width),
                grad_values.reshape(row_count, key_block, model_width),
            ],
            axis=-1,
        )
        key_terms = lax.dynamic_update_slice_in_dim(key_terms, both_terms, start, 1)
        return (grad_query, key_terms)

    term_start = jnp.zeros((row_count, frame_count, 2 * model_width), jnp.float32)
    return lax.fori_loop(
        0, block_count, back_step, (jnp.zeros(query_heads.shape, jnp.float32), term_start)
    )


def local(
    features,
    cotangent,
    segments,
    stem_weight,
    projection_weight,
    mixing_weight,
    feedforward_weight,
    norm_gains,
    biases,
    stem_moment,
    projection_moment,
    mixing_moment,
    feedforward_moment,
    gain_moment,
    bias_moment,
    stem_average,
    projection_average,
    mixing_average,
    feedforward_average,
    gain_average,
    bias_average,
):
    row_count, tok_count, model_width = features.shape
    head_count = HEADS
    head_width = model_width // head_count
    group_count = GROUPS
    group_width = model_width // group_count
    tap_count = KERNEL
    half_taps = tap_count // 2
    layer_count = projection_weight.shape[0]
    ff_rows = feedforward_weight.shape[3] // model_width
    score_scale = 1.0 / math.sqrt(head_width)
    seq_index = lax.axis_index("seq")
    query_segments = lax.dynamic_slice_in_dim(segments, seq_index * tok_count, tok_count, 1)
    kernel_taps = stem_weight.reshape(tap_count, group_width, model_width)
    extended = extended_2(features, (("seq", 1),), half_taps)
    conv_input = extended[:, : tok_count + tap_count - 1]
    conv_pre = group_conv(conv_input, kernel_taps, group_count) + biases[0]
    summed = features.astype(jnp.float32) + gelu_exact(conv_pre)
    hidden, normed_stem, inverse_stem = layer_norm(summed, norm_gains[0], biases[1])
    saved_layers = []
    for layer_index in range(layer_count):
        bias_base = 2 + layer_index * (6 + ff_rows)
        hidden_low = hidden.astype(jnp.bfloat16)
        projected = jnp.einsum(
            "rtd,de->rte",
            hidden_low,
            projection_weight[layer_index],
            preferred_element_type=jnp.float32,
        )
        queries = ((projected[..., :model_width] + biases[bias_base]) * score_scale).astype(
            jnp.bfloat16
        )
        keys_low = projected[..., model_width : 2 * model_width].astype(jnp.bfloat16)
        values_low = (projected[..., 2 * model_width :] + biases[bias_base + 1]).astype(
            jnp.bfloat16
        )
        kv_local = jnp.concatenate([keys_low, values_low], axis=-1)
        kv_whole = lax.all_gather(kv_local, "seq", axis=1, tiled=True)
        query_heads = queries.reshape(row_count, tok_count, head_count, head_width)
        coarse, fine, log_sum = attend(query_heads, kv_whole, query_segments, segments, head_count)
        mixed_low = coarse.reshape(row_count, tok_count, model_width).astype(jnp.bfloat16)
        branch = (
            jnp.einsum(
                "rte,ed->rtd",
                mixed_low,
                mixing_weight[layer_index],
                preferred_element_type=jnp.float32,
            )
            + biases[bias_base + 2]
        )
        first_norm, normed_one, inverse_one = layer_norm(
            hidden + branch, norm_gains[1 + 2 * layer_index], biases[bias_base + 3]
        )
        first_low = first_norm.astype(jnp.bfloat16)
        up_bias = biases[bias_base + 6 : bias_base + 6 + ff_rows].reshape(-1)
        up_pre = (
            jnp.einsum(
                "rtd,dj->rtj",
                first_low,
                feedforward_weight[layer_index, :, 0, :],
                preferred_element_type=jnp.float32,
            )
            + up_bias
        )
        up_low = gelu_exact(up_pre).astype(jnp.bfloat16)
        down_out = (
            jnp.einsum(
                "rtj,dj->rtd",
                up_low,
                feedforward_weight[layer_index, :, 1, :],
                preferred_element_type=jnp.float32,
            )
            + biases[bias_base + 4]
        )
        hidden_next, normed_two, inverse_two = layer_norm(
            first_norm + down_out, norm_gains[2 + 2 * layer_index], biases[bias_base + 5]
        )
        saved_layers.append(
            (
                hidden_low,
                query_heads,
                kv_whole,
                log_sum,
                fine,
                mixed_low,
                normed_one,
                inverse_one,
                first_low,
                up_pre,
                up_low,
                normed_two,
                inverse_two,
            )
        )
        hidden = hidden_next
    upstream = cotangent.astype(jnp.float32)
    gain_grads = [None] * norm_gains.shape[0]
    bias_grads = [None] * biases.shape[0]
    projection_grads = [None] * layer_count
    mixing_grads = [None] * layer_count
    feedforward_grads = [None] * layer_count
    for layer_index in reversed(range(layer_count)):
        (
            hidden_low,
            query_heads,
            kv_whole,
            log_sum,
            fine,
            mixed_low,
            normed_one,
            inverse_one,
            first_low,
            up_pre,
            up_low,
            normed_two,
            inverse_two,
        ) = saved_layers[layer_index]
        bias_base = 2 + layer_index * (6 + ff_rows)
        in_matrix = projection_weight[layer_index]
        mix_matrix = mixing_weight[layer_index]
        up_matrix = feedforward_weight[layer_index, :, 0, :]
        down_matrix = feedforward_weight[layer_index, :, 1, :]
        grad_second, gain_grads[2 + 2 * layer_index], bias_grads[bias_base + 5] = layer_norm_back(
            upstream, normed_two, inverse_two, norm_gains[2 + 2 * layer_index]
        )
        bias_grads[bias_base + 4] = jnp.sum(grad_second, axis=(0, 1))
        down_low = grad_second.astype(jnp.bfloat16)
        grad_down = jnp.einsum("rtd,rtj->dj", down_low, up_low, preferred_element_type=jnp.float32)
        grad_act = jnp.einsum(
            "rtd,dj->rtj", down_low, down_matrix, preferred_element_type=jnp.float32
        )
        grad_up_pre = gelu_back(up_pre, grad_act)
        up_bias_grad = jnp.sum(grad_up_pre, axis=(0, 1)).reshape(ff_rows, model_width)
        for offset in range(ff_rows):
            bias_grads[bias_base + 6 + offset] = up_bias_grad[offset]
        up_grad_low = grad_up_pre.astype(jnp.bfloat16)
        grad_up = jnp.einsum(
            "rtd,rtj->dj", first_low, up_grad_low, preferred_element_type=jnp.float32
        )
        grad_first = grad_second + jnp.einsum(
            "rtj,dj->rtd", up_grad_low, up_matrix, preferred_element_type=jnp.float32
        )
        feedforward_grads[layer_index] = jnp.stack([grad_up, grad_down], axis=1)
        grad_resid, gain_grads[1 + 2 * layer_index], bias_grads[bias_base + 3] = layer_norm_back(
            grad_first, normed_one, inverse_one, norm_gains[1 + 2 * layer_index]
        )
        bias_grads[bias_base + 2] = jnp.sum(grad_resid, axis=(0, 1))
        branch_low = grad_resid.astype(jnp.bfloat16)
        mixing_grads[layer_index] = jnp.einsum(
            "rte,rtd->ed", mixed_low, branch_low, preferred_element_type=jnp.float32
        )
        grad_mixed = jnp.einsum(
            "rtd,ed->rte", branch_low, mix_matrix, preferred_element_type=jnp.float32
        )
        mixed_grad_low = grad_mixed.astype(jnp.bfloat16).reshape(
            row_count, tok_count, head_count, head_width
        )
        delta = jnp.transpose(
            jnp.sum(mixed_grad_low.astype(jnp.float32) * fine, axis=-1), (0, 2, 1)
        )
        grad_query, key_terms = attend_back(
            query_heads,
            mixed_grad_low,
            kv_whole,
            query_segments,
            segments,
            log_sum,
            delta,
            head_count,
        )
        grad_kv = lax.psum_scatter(key_terms, "seq", scatter_dimension=1, tiled=True)
        query_grad_low = grad_query.reshape(row_count, tok_count, model_width).astype(jnp.bfloat16)
        key_grad_low = grad_kv[..., :model_width].astype(jnp.bfloat16)
        value_grad_low = grad_kv[..., model_width:].astype(jnp.bfloat16)
        bias_grads[bias_base] = (
            jnp.sum(query_grad_low.astype(jnp.float32), axis=(0, 1)) * score_scale
        )
        bias_grads[bias_base + 1] = jnp.sum(value_grad_low.astype(jnp.float32), axis=(0, 1))
        grad_projected = jnp.concatenate(
            [query_grad_low * score_scale, key_grad_low, value_grad_low], axis=-1
        )
        projection_grads[layer_index] = jnp.einsum(
            "rtd,rte->de", hidden_low, grad_projected, preferred_element_type=jnp.float32
        )
        upstream = grad_resid + jnp.einsum(
            "rte,de->rtd", grad_projected, in_matrix, preferred_element_type=jnp.float32
        )
    grad_summed, gain_grads[0], bias_grads[1] = layer_norm_back(
        upstream, normed_stem, inverse_stem, norm_gains[0]
    )
    grad_conv = gelu_back(conv_pre, grad_summed)
    bias_grads[0] = jnp.sum(grad_conv, axis=(0, 1))
    conv_grad_low = grad_conv.astype(jnp.bfloat16)
    grad_extended = extended_2(conv_grad_low, (("seq", 1),), half_taps)
    features_gradient = grad_summed + group_conv(
        grad_extended[:, 1:], flipped_taps(kernel_taps, group_count), group_count
    )
    seq_count = lax.axis_size("seq")
    share_width = model_width // seq_count
    layer_partials = (
        jnp.stack(projection_grads),
        jnp.stack(mixing_grads),
        jnp.stack(feedforward_grads),
        jnp.stack(gain_grads),
        jnp.stack(bias_grads),
    )
    grad_stem = group_conv_kernel_grad(conv_input, conv_grad_low, group_count).reshape(
        tap_count * group_width, model_width
    )
    shares = (
        lax.psum_scatter(grad_stem, "seq", scatter_dimension=1, tiled=True),
        lax.psum_scatter(layer_partials[0], "seq", scatter_dimension=1, tiled=True),
        lax.psum_scatter(layer_partials[1], "seq", scatter_dimension=1, tiled=True),
        lax.psum_scatter(layer_partials[2], "seq", scatter_dimension=1, tiled=True),
        lax.psum_scatter(layer_partials[3], "seq", scatter_dimension=1, tiled=True),
        lax.psum_scatter(layer_partials[4], "seq", scatter_dimension=1, tiled=True),
    )
    matrix_totals = (
        lax.psum_scatter(
            shares[0].astype(jnp.bfloat16), "row", scatter_dimension=0, tiled=True
        ).astype(jnp.float32),
        lax.psum_scatter(
            shares[1].astype(jnp.bfloat16), "row", scatter_dimension=2, tiled=True
        ).astype(jnp.float32),
        lax.psum_scatter(
            shares[2].astype(jnp.bfloat16), "row", scatter_dimension=2, tiled=True
        ).astype(jnp.float32),
        lax.psum_scatter(
            shares[3].astype(jnp.bfloat16), "row", scatter_dimension=3, tiled=True
        ).astype(jnp.float32),
    )
    small_totals = lax.psum((shares[4], shares[5]), "row")
    totals = (
        matrix_totals[0],
        matrix_totals[1],
        matrix_totals[2],
        matrix_totals[3],
        small_totals[0],
        small_totals[1],
    )
    share_start = seq_index * share_width
    row_index = lax.axis_index("row")
    row_total = lax.axis_size("row")
    rate_base = 1.0 / math.sqrt(row_count * row_total * tok_count * seq_count)
    old_params = (
        stem_weight,
        projection_weight,
        mixing_weight,
        feedforward_weight,
        norm_gains,
        biases,
    )
    old_moments = (
        stem_moment,
        projection_moment,
        mixing_moment,
        feedforward_moment,
        gain_moment,
        bias_moment,
    )
    old_averages = (
        stem_average,
        projection_average,
        mixing_average,
        feedforward_average,
        gain_average,
        bias_average,
    )
    momenta = []
    averaged = []
    updated = []
    for param_index in range(6):
        old_share = lax.dynamic_slice_in_dim(old_params[param_index], share_start, share_width, 1)
        if param_index < 4:
            split_dim = row_dims[param_index]
            piece_size = old_share.shape[split_dim] // row_total
            old_share = lax.dynamic_slice_in_dim(
                old_share, row_index * piece_size, piece_size, split_dim
            )
        old_share = old_share.astype(jnp.float32)
        moment_new = momentum_decay * old_moments[param_index] + totals[param_index]
        weight_new = old_share - rate_factors[param_index] * rate_base * (
            totals[param_index] + momentum_decay * moment_new
        )
        momenta.append(moment_new)
        updated.append(weight_new)
        averaged.append(
            average_decay * old_averages[param_index] + (1.0 - average_decay) * weight_new
        )
    return (
        hidden,
        features_gradient,
        momenta[0],
        momenta[1],
        momenta[2],
        momenta[3],
        momenta[4],
        momenta[5],
        averaged[0],
        averaged[1],
        averaged[2],
        averaged[3],
        averaged[4],
        averaged[5],
        updated[0],
        updated[1],
        updated[2],
        updated[3],
        updated[4],
        updated[5],
    )


def solution(mesh):
    in_specs = (
        P("row", "seq", None),
        P("row", "seq", None),
        P("row", None),
        P(),
        P(),
        P(),
        P(),
        P(),
        P(),
        P("row", "seq"),
        P(None, "seq", "row"),
        P(None, "seq", "row"),
        P(None, "seq", None, "row"),
        P(None, "seq"),
        P(None, "seq"),
        P("row", "seq"),
        P(None, "seq", "row"),
        P(None, "seq", "row"),
        P(None, "seq", None, "row"),
        P(None, "seq"),
        P(None, "seq"),
    )
    out_specs = (
        P("row", "seq", None),
        P("row", "seq", None),
        P("row", "seq"),
        P(None, "seq", "row"),
        P(None, "seq", "row"),
        P(None, "seq", None, "row"),
        P(None, "seq"),
        P(None, "seq"),
        P("row", "seq"),
        P(None, "seq", "row"),
        P(None, "seq", "row"),
        P(None, "seq", None, "row"),
        P(None, "seq"),
        P(None, "seq"),
        P("row", "seq"),
        P(None, "seq", "row"),
        P(None, "seq", "row"),
        P(None, "seq", None, "row"),
        P(None, "seq"),
        P(None, "seq"),
    )
    return jax.shard_map(local, mesh=mesh, in_specs=in_specs, out_specs=out_specs, check_vma=False)
```

profile of v0, /device:TPU:0, one launch (start us, length us, event | category | flops | bytes accessed | tf_op | source)
XLA Modules:
  0.0 2117.3 jit_solution(10378962256239727422)
XLA Ops:
  15.4 35.2 %reshape.325 = bf16[128,48,16,48]{3,2,1,0:T(8,128)(2,1)} reshape(bf16[6144,768]{1,0:T(8,128)(2,1)} %param.24) | data formatting | bytes 18874368 | tf_op jit(solution)/shard_map/reshape | solution.py:245
  55.0 35.9 %fusion = f32[2,64,16,48]{3,0,2,1:T(2,128)S(1)} fusion(bf16[2,191,16,48]{3,0,2,1:T(2,128)(2,1)S(1)} %copy.136, bf16[128,48,16,48]{3,2,1,0:T(8,128)(2,1)} %reshape.325), kind=kOutput, calls=%fused_computation.1 | convolution fusion | flops 1207959552 | bytes 10417152 | tf_op jit(solution)/shard_map/conv_general_dilated | solution.py:65
  99.6 36.2 %fusion.171 = (bf16[1,768,1,3072]{3,2,1,0:T(2,128)(2,1)}, bf16[1,768,1,3072]{3,2,1,0:T(2,128)(2,1)}, bf16[1,768,1,3072]{3,2,1,0:T(2,128)(2,1)}, bf16[1,768,1,3072]{3,2,1,0:T(2,128)(2,1)}) fusion(bf16[2,768,2,3072]{3,2,1,0:T(2,128)(2,1)} %param.27), kind=kLoop, calls=%fused_computation.339 | loop fusion | bytes 37748736 | tf_op jit(solution)/shard_map/slice | solution.py:291
  136.7 22.3 %all-gather.3.cloned.1.call-done = bf16[2,512,1536]{2,1,0:T(8,128)(2,1)} async-done(((bf16[2,64,1536]{2,1,0:T(8,128)(2,1)}), bf16[2,512,1536]{2,1,0:T(8,128)(2,1)}) %all-gather.3.cloned.1.call-update) | async-done | bytes 3145744 | tf_op jit(solution)/shard_map/all_gather | solution.py:269
  170.5 6.1 fusion.124
  188.0 56.0 %all-gather.5.cloned.1.call-done = bf16[2,512,1536]{2,1,0:T(8,128)(2,1)} async-done(((bf16[2,64,1536]{2,1,0:T(8,128)(2,1)}), bf16[2,512,1536]{2,1,0:T(8,128)(2,1)}) %all-gather.5.cloned.1.call-update) | async-done | bytes 3145744 | tf_op jit(solution)/shard_map/all_gather | solution.py:269
  260.5 6.1 fusion.125
  266.7 9.6 fusion.182
  276.9 6.2 fusion.184
  309.7 6.2 pad_maximum_fusion.2
  322.2 110.5 %reduce-scatter.23.cloned.1.call-done = f32[2,64,1536]{2,1,0:T(8,128)} async-done(((f32[2,512,1536]{2,1,0:T(8,128)}), f32[2,64,1536]{2,1,0:T(8,128)}) %reduce-scatter.23.cloned.1.call-update) | async-done | bytes 786448 | tf_op jit(solution)/shard_map/reduce_scatter | solution.py:402
  439.2 9.6 fusion.183
  472.4 6.2 pad_maximum_fusion.3
  491.2 104.7 %reduce-scatter.25.cloned.1.call-done = f32[2,64,1536]{2,1,0:T(8,128)} async-done(((f32[2,512,1536]{2,1,0:T(8,128)}), f32[2,64,1536]{2,1,0:T(8,128)}) %reduce-scatter.25.cloned.1.call-update) | async-done | bytes 786448 | tf_op jit(solution)/shard_map/reduce_scatter | solution.py:402
  607.9 10.9 pad_maximum_fusion.1
  620.2 74.7 %fusion.88 = f32[128,48,16,48]{3,1,2,0:T(8,128)} fusion(bf16[2,191,16,48]{3,0,2,1:T(2,128)(2,1)S(1)} %copy-done.56, bf16[2,64,16,48]{3,2,1,0:T(8,128)(2,1)S(1)} %convert_element_type.240), kind=kOutput, calls=%fused_computation.165 | convolution fusion | flops 1207959552 | bytes 19657728 | tf_op jit(solution)/shard_map/conv_general_dilated | solution.py:77
  694.9 53.8 %copy.200 = f32[128,48,16,48]{1,0,3,2:T(8,128)} copy(f32[128,48,16,48]{3,1,2,0:T(8,128)} %fusion.88) | data formatting | bytes 37748736
  748.7 47.5 %reshape.366 = f32[6144,768]{0,1:T(8,128)} reshape(f32[128,48,16,48]{1,0,3,2:T(8,128)} %copy.200) | data formatting | bytes 37748736
  804.4 7.1 maximum_bitcast_fusion.1
  817.2 6.8 convolution_bitcast_fusion.2
  826.6 13.1 maximum_bitcast_fusion
  842.0 28.6 %pad_maximum_fusion = f32[2,768,2,3072]{3,1,2,0:T(8,128)} fusion(f32[1,768,2,3072]{3,1,2,0:T(8,128)} %maximum_bitcast_fusion.1, f32[1,768,2,3072]{3,1,2,0:T(8,128)} %maximum_bitcast_fusion), kind=kLoop, calls=%fused_computation | loop fusion | flops 9437184 | bytes 75497472 | tf_op jit(solution)/shard_map/stack | solution.py:434
  870.7 55.6 %reduce-scatter.29.cloned.1.call-done = f32[2,96,2304]{2,1,0:T(8,128)} async-done(((f32[2,768,2304]{2,1,0:T(8,128)}), f32[2,96,2304]{2,1,0:T(8,128)}) %reduce-scatter.29.cloned.1.call-update) | async-done | bytes 1769488 | tf_op jit(solution)/shard_map/reduce_scatter | solution.py:443
  931.3 311.4 %reduce-scatter.37.cloned.1.call-done = f32[96,6144]{1,0:T(8,128)} async-done(((f32[768,6144]{1,0:T(8,128)}), f32[96,6144]{1,0:T(8,128)}) %reduce-scatter.37.cloned.1.call-update) | async-done | bytes 2359312
  1248.9 40.1 %copy.164 = bf16[128,48,16,48]{0,3,2,1:T(8,128)(2,1)} copy(bf16[128,48,16,48]{1,2,3,0:T(8,128)(2,1)} %bitcast.225) | data formatting | bytes 18874368 | tf_op jit(solution)/shard_map/transpose | solution.py:91
  1289.0 140.0 %rev.5 = bf16[128,48,768]{0,2,1:T(8,128)(2,1)} reverse(bf16[128,48,768]{0,2,1:T(8,128)(2,1)} %bitcast.227), dimensions={0} | reverse | bytes 18874368 | tf_op jit(solution)/shard_map/rev | solution.py:92
  1429.0 33.8 %copy.166 = bf16[128,48,16,48]{3,1,2,0:T(8,128)(2,1)} copy(bf16[128,48,16,48]{0,3,2,1:T(8,128)(2,1)} %bitcast.228) | data formatting | bytes 18874368 | tf_op jit(solution)/shard_map/rev | solution.py:92
  1476.7 11.1 all-reduce
  1493.3 514.8 %reduce-scatter.33.cloned.1.call-done = f32[2,96,2,3072]{3,1,2,0:T(8,128)} async-done(((f32[2,768,2,3072]{3,1,2,0:T(8,128)}), f32[2,96,2,3072]{3,1,2,0:T(8,128)}) %reduce-scatter.33.cloned.1.call-update) | async-done | bytes 4718608 | tf_op jit(solution)/shard_map/reduce_scatter | solution.py:445
  2012.2 35.7 %fusion.185 = f32[2,64,16,48]{3,0,2,1:T(2,128)S(1)} fusion(bf16[2,191,16,48]{3,0,2,1:T(2,128)(2,1)S(1)} %copy.165, bf16[128,48,16,48]{3,1,2,0:T(8,128)(2,1)} %copy.166), kind=kOutput, calls=%fused_computation.353 | convolution fusion | flops 1207959552 | bytes 10417152 | tf_op jit(solution)/shard_map/conv_general_dilated | solution.py:65
  2053.9 13.0 reduce-scatter.27.cloned.1.call-done
  2073.8 28.7 %reduce-scatter.35.cloned.1.call-done = bf16[2,96,2,768]{3,1,2,0:T(8,128)(2,1)} async-done(((bf16[2,96,2,3072]{3,1,2,0:T(8,128)(2,1)}), bf16[2,96,2,768]{3,1,2,0:T(8,128)(2,1)}) %reduce-scatter.35.cloned.1.call-update) | async-done | bytes 589840 | tf_op jit(solution)/shard_map/reduce_scatter | solution.py:459
  (618 shorter events, 222.7 us)
Async XLA Ops:
  7.2 151.8 %all-gather.3.cloned.1.call-start = ((), (), s32[]{:S(2)}) async-start(), calls=%async_computation.12 | async-start | bytes 3538944 | tf_op jit(solution)/shard_map/all_gather | solution.py:269
  8.4 42.1 %copy-start.94 = (f32[22,768]{1,0:T(8,128)S(1)}, f32[22,768]{1,0:T(8,128)}, u32[]{:S(2)}) copy-start(f32[22,768]{1,0:T(8,128)} %param.29) | copy-start | bytes 202756
  8.4 42.1 %copy-start.141 = (f32[5,768]{1,0:T(8,128)S(1)}, f32[5,768]{1,0:T(8,128)}, u32[]{:S(2)}) copy-start(f32[5,768]{1,0:T(8,128)} %param.28) | copy-start | bytes 46084
  8.4 42.9 %collective-permute-start.1 = (bf16[2,64,768]{1,2,0:T(8,128)(2,1)S(1)}, bf16[2,64,768]{1,2,0:T(8,128)(2,1)S(1)}, u32[]{:S(2)}, u32[]{:S(2)}) collective-permute-start(bf16[2,64,768]{1,2,0:T(8,128)(2,1)S(1)} %copy.133), channel_id=1, source_target_pairs={{1,0},{2,1},{3,2},{4,3},{5,4},{6,5},{7,6},{9,8},{10,9},{11,10},{12... | collective-permute-start | bytes 589832 | tf_op jit(solution)/shard_map/ppermute | solution.py:31
  9.8 41.4 %collective-permute-start = (bf16[2,64,768]{1,2,0:T(8,128)(2,1)S(1)}, bf16[2,64,768]{1,2,0:T(8,128)(2,1)S(1)}, u32[]{:S(2)}, u32[]{:S(2)}) collective-permute-start(bf16[2,64,768]{1,2,0:T(8,128)(2,1)S(1)} %copy.133), channel_id=1, source_target_pairs={{0,1},{1,2},{2,3},{3,4},{4,5},{5,6},{6,7},{8,9},{9,10},{10,11},{11... | collective-permute-start | bytes 589832 | tf_op jit(solution)/shard_map/ppermute | solution.py:29
  92.8 510.9 %copy-start.2 = (f32[2,64,768]{2,1,0:T(8,128)}, f32[2,64,768]{2,1,0:T(8,128)S(1)}, u32[]{:S(2)}) copy-start(f32[2,64,768]{2,1,0:T(8,128)S(1)} %get-tuple-element.319) | copy-start | bytes 1179652
  92.8 76.8 %copy-start.95 = (f32[2,64]{1,0:T(2,128)}, f32[2,64]{1,0:T(2,128)S(1)}, u32[]{:S(2)}) copy-start(f32[2,64]{1,0:T(2,128)S(1)} %broadcast_multiply_fusion.16) | copy-start | bytes 1540
  96.7 147.3 %all-gather.5.cloned.1.call-start = ((), (), s32[]{:S(2)}) async-start(), calls=%async_computation.13 | async-start | bytes 3538944 | tf_op jit(solution)/shard_map/all_gather | solution.py:269
  184.8 247.9 %reduce-scatter.23.cloned.1.call-start = ((), (), s32[]{:S(2)}) async-start(), calls=%async_computation.14 | async-start | bytes 7077888 | tf_op jit(solution)/shard_map/reduce_scatter | solution.py:402
  260.2 25.6 %copy-start.21 = (f32[2,64,768]{2,1,0:T(8,128)}, f32[2,64,768]{2,1,0:T(8,128)S(1)}, u32[]{:S(2)}) copy-start(f32[2,64,768]{2,1,0:T(8,128)S(1)} %get-tuple-element.359) | copy-start | bytes 1179652
  260.2 25.5 %copy-start.119 = (f32[2,64]{1,0:T(2,128)}, f32[2,64]{1,0:T(2,128)S(1)}, u32[]{:S(2)}) copy-start(f32[2,64]{1,0:T(2,128)S(1)} %broadcast_multiply_fusion.13) | copy-start | bytes 1540
  260.4 25.3 %copy-start.126 = (f32[2,64]{1,0:T(2,128)}, f32[2,64]{1,0:T(2,128)S(1)}, u32[]{:S(2)}) copy-start(f32[2,64]{1,0:T(2,128)S(1)} %add_rsqrt_fusion.1) | copy-start | bytes 1540
  315.9 280.1 %reduce-scatter.25.cloned.1.call-start = ((), (), s32[]{:S(2)}) async-start(), calls=%async_computation.15 | async-start | bytes 7077888 | tf_op jit(solution)/shard_map/reduce_scatter | solution.py:402
  478.7 345.2 %reduce-scatter.31.cloned.1.call-start = ((), (), s32[]{:S(2)}) async-start(), calls=%async_computation.18 | async-start | bytes 5308416 | tf_op jit(solution)/shard_map/reduce_scatter | solution.py:444
  483.4 442.9 %reduce-scatter.29.cloned.1.call-start = ((), (), s32[]{:S(2)}) async-start(), calls=%async_computation.17 | async-start | bytes 15925248 | tf_op jit(solution)/shard_map/reduce_scatter | solution.py:443
  487.1 110.0 %copy-start.38 = (f32[2,64,768]{2,1,0:T(8,128)S(1)}, f32[2,64,768]{2,1,0:T(8,128)}, u32[]{:S(2)}) copy-start(f32[2,64,768]{2,1,0:T(8,128)} %copy-done.36) | copy-start | bytes 1179652
  487.1 110.0 %copy-start.96 = (f32[2,64]{1,0:T(2,128)S(1)}, f32[2,64]{1,0:T(2,128)}, u32[]{:S(2)}) copy-start(f32[2,64]{1,0:T(2,128)} %copy-done.95) | copy-start | bytes 1540
  487.2 110.0 %copy-start.104 = (f32[2,64]{1,0:T(2,128)S(1)}, f32[2,64]{1,0:T(2,128)}, u32[]{:S(2)}) copy-start(f32[2,64]{1,0:T(2,128)} %copy-done.102) | copy-start | bytes 1540
  618.8 623.9 %reduce-scatter.37.cloned.1.call-start = ((), (), s32[]{:S(2)}) async-start(), calls=%async_computation.21 | async-start | bytes 21233664
  796.4 669.7 %reduce-scatter.41.cloned.1.call-start = ((), (), s32[]{:S(2)}) async-start(), calls=%async_computation.23 | async-start | bytes 491520
  826.5 648.4 %reduce-scatter.43.cloned.1.call-start = ((), (), s32[]{:S(2)}) async-start(), calls=%async_computation.24 | async-start | bytes 442368
  840.7 635.1 %reduce-scatter.45.cloned.1.call-start = ((), (), s32[]{:S(2)}) async-start(), calls=%async_computation.25 | async-start | bytes 442368
  842.0 1166.1 %reduce-scatter.33.cloned.1.call-start = ((), (), s32[]{:S(2)}) async-start(), calls=%async_computation.19 | async-start | bytes 42467328 | tf_op jit(solution)/shard_map/reduce_scatter | solution.py:445
  870.7 1179.3 %reduce-scatter.39.cloned.1.call-start = ((), (), s32[]{:S(2)}) async-start(), calls=%async_computation.22 | async-start | bytes 1474560
  931.3 1135.6 %reduce-scatter.27.cloned.1.call-start = ((), (), s32[]{:S(2)}) async-start(), calls=%async_computation.16 | async-start | bytes 1966080 | tf_op jit(solution)/shard_map/reduce_scatter | solution.py:450
  1245.5 857.0 %reduce-scatter.35.cloned.1.call-start = ((), (), s32[]{:S(2)}) async-start(), calls=%async_computation.20 | async-start | bytes 2949120 | tf_op jit(solution)/shard_map/reduce_scatter | solution.py:459
  1462.8 25.0 %copy-start.144 = (f32[22,96]{1,0:T(8,128)S(1)}, f32[22,96]{1,0:T(8,128)}, u32[]{:S(2)}) copy-start(f32[22,96]{1,0:T(8,128)} %param.41) | copy-start | bytes 25348
  1462.8 26.4 %copy-start.153 = (f32[5,96]{1,0:T(8,128)S(1)}, f32[5,96]{1,0:T(8,128)}, u32[]{:S(2)}) copy-start(f32[5,96]{1,0:T(8,128)} %param.40) | copy-start | bytes 5764
  1462.8 26.4 %copy-start.154 = (f32[5,96]{1,0:T(8,128)S(1)}, f32[5,96]{1,0:T(8,128)}, u32[]{:S(2)}) copy-start(f32[5,96]{1,0:T(8,128)} %param.34) | copy-start | bytes 5764
  1469.1 21.6 %collective-permute-start.3 = (bf16[2,64,768]{2,1,0:T(8,128)(2,1)S(1)}, bf16[2,64,768]{2,1,0:T(8,128)(2,1)S(1)}, u32[]{:S(2)}, u32[]{:S(2)}) collective-permute-start(bf16[2,64,768]{2,1,0:T(8,128)(2,1)S(1)} %copy-done.52), channel_id=1, source_target_pairs={{1,0},{2,1},{3,2},{4,3},{5,4},{6,5},{7,6},{9,8},{10,9},{11,10},{12... | collective-permute-start | bytes 589832 | tf_op jit(solution)/shard_map/ppermute | solution.py:31
  1470.4 20.3 collective-permute-start.2
  2071.7 30.9 %copy-start.50 = (bf16[2,96,2,768]{3,2,1,0:T(2,128)(2,1)S(1)}, bf16[2,96,2,768]{3,2,1,0:T(2,128)(2,1)}, u32[]{:S(2)}) copy-start(bf16[2,96,2,768]{3,2,1,0:T(2,128)(2,1)} %constant_dynamic-slice_fusion) | copy-start | bytes 1769476
  (181 other events, 841.7 us)
Sparse Core Ops, SparseCore 0:
  96.8 62.0 all-gather.2
  184.9 59.0 all-gather.4
  316.0 116.5 reduce-scatter.22
  478.8 117.0 reduce-scatter.24
  599.5 94.3 reduce-scatter.30
  697.4 228.8 reduce-scatter.28
  930.2 312.4 reduce-scatter.36
  1245.8 19.9 reduce-scatter.40
  1269.6 61.4 reduce-scatter.42
  1334.8 60.6 reduce-scatter.44
  1399.3 608.6 reduce-scatter.32
  2011.2 24.8 reduce-scatter.38
  2038.7 28.1 reduce-scatter.26
  2069.4 33.0 reduce-scatter.34
where the time goes:
time: 2140 us; the launch traced here: 2120 us
  waiting for transfers between devices  1220 us (57%)
  local copies, waits for them, and re-layouts  479 us (22%)
  matrix products  269 us (13%)
  other arithmetic  110 us (5%)
    reduce_scatter x1, waiting for transfers between devices, local(): lax.psum_scatter(layer_partials[2], 'seq', scatter_dimension=1, tiled=True)  515 us
    unnamed x19, waiting for transfers between devices  312 us
    reduce_scatter x2, waiting for transfers between devices, local(): lax.psum_scatter(key_terms, 'seq', scatter_dimension=1, tiled=True)  215 us
    rev x2, local copies, waits for them, and re-layouts, flipped_taps(): return swapped[::-1]  174 us
    unnamed x414, local copies, waits for them, and re-layouts  141 us
    all_gather x2, waiting for transfers between devices, local(): kv_whole = lax.all_gather(kv_local, 'seq', axis=1, tiled=True)  78.3 us
    conv_general_dilated x1, matrix products, group_conv_kernel_grad(): lax.conv_general_dilated(extended, upstream_low, (1,), 'VALID', dimension...  74.7 us
    conv_general_dilated x2, matrix products, group_conv(): lax.conv_general_dilated(extended, kernel_taps, (1,), 'VALID', dimension_...  71.6 us
  transfers between devices with their start and end apart: 18, of which 9 were waited for; matrix products, arithmetic and copies ran while one was open for 31% of the time, Pallas kernels for 0%

commit v1 on v0

--- a/solution.py
+++ b/solution.py
@@ -1,8 +1,12 @@
+import functools
 import math
 
 import jax
 import jax.numpy as jnp
 from jax import lax
+from jax.experimental import pallas as pl
+from jax.experimental.pallas import tpu as pltpu
+from jax.sharding import Mesh
 from jax.sharding import PartitionSpec as P
 
 HEADS = 12
@@ -542,50 +546,882 @@
     )
 
 
+LANES = 128
+PAIRS = 2
+VMEM_BYTES = 48 * 1024 * 1024
+bf16 = jnp.bfloat16
+f32 = jnp.float32
+
+
+def whole_call(kernel, outs, operands, scalars=0, scratch=(), flops=0, moved=0):
+    in_specs = [
+        pl.BlockSpec(memory_space=pltpu.SMEM if i < scalars else pltpu.VMEM)
+        for i in range(len(operands))
+    ]
+    many = isinstance(outs, (list, tuple))
+    out_specs = [pl.BlockSpec(memory_space=pltpu.VMEM) for _ in outs] if many else pl.BlockSpec(memory_space=pltpu.VMEM)
+    shapes = list(outs) if many else [outs]
+    size = sum(math.prod(o.shape) * o.dtype.itemsize for o in shapes) + sum(
+        math.prod(o.shape) * o.dtype.itemsize for o in operands
+    )
+    return pl.pallas_call(
+        kernel,
+        out_shape=list(outs) if many else outs,
+        in_specs=in_specs,
+        out_specs=out_specs,
+        scratch_shapes=list(scratch),
+        compiler_params=pltpu.CompilerParams(vmem_limit_bytes=VMEM_BYTES),
+        cost_estimate=pl.CostEstimate(flops=int(flops), bytes_accessed=int(size), transcendentals=0),
+    )(*operands)
+
+
+def sds(shape, dtype):
+    return jax.ShapeDtypeStruct(shape, dtype)
+
+
+def dot_nn(a, b):
+    return lax.dot_general(a, b, (((1,), (0,)), ((), ())), preferred_element_type=f32)
+
+
+def dot_nt(a, b):
+    return lax.dot_general(a, b, (((1,), (1,)), ((), ())), preferred_element_type=f32)
+
+
+def dot_tn(a, b):
+    return lax.dot_general(a, b, (((0,), (0,)), ((), ())), preferred_element_type=f32)
+
+
+def gelu_and_slope(v):
+    cdf = 0.5 * (1.0 + lax.erf(v * math.sqrt(0.5)))
+    return v * cdf, cdf + v * jnp.exp(-0.5 * v * v) * (1.0 / math.sqrt(2.0 * math.pi))
+
+
+def lane_of(shape):
+    return lax.broadcasted_iota(jnp.int32, shape, len(shape) - 1)
+
+
+def piece_of(cols, j, width):
+    off, v = (width * j) % LANES, (width * j) // LANES
+    lane = lane_of(cols[0].shape)
+    if off == 0:
+        t = cols[v]
+    else:
+        t = pltpu.roll(cols[v], LANES - off, 1)
+        if off + width > LANES:
+            t = jnp.where(lane < LANES - off, t, pltpu.roll(cols[v + 1], LANES - off, 1))
+    return jnp.where(lane < width, t, 0.0)
+
+
+def tiles_of(pieces, width):
+    count = len(pieces) * width // LANES
+    cols = [None] * count
+
+    def put(v, t):
+        cols[v] = t if cols[v] is None else cols[v] + t
+
+    for j, piece in enumerate(pieces):
+        off, v = (width * j) % LANES, (width * j) // LANES
+        if off == 0:
+            put(v, piece)
+            continue
+        rolled = pltpu.roll(piece, off, 1)
+        if off + width > LANES:
+            lane = lane_of(piece.shape)
+            put(v, jnp.where(lane >= off, rolled, 0.0))
+            put(v + 1, jnp.where(lane < off, rolled, 0.0))
+        else:
+            put(v, rolled)
+    return cols
+
+
+def split_kernel(blocks, width, x_ref, o_ref):
+    rows = x_ref.shape[0]
+    for r in range(rows):
+        x = x_ref[r].astype(f32)
+        cols = [x[:, LANES * v : LANES * (v + 1)] for v in range(x.shape[1] // LANES)]
+        for j in range(blocks):
+            o_ref[j, r] = piece_of(cols, j, width).astype(bf16)
+
+
+def taps_kernel(taps, gw, w_ref, o_ref):
+    zero = jnp.zeros((LANES, LANES), bf16)
+    o_ref[0] = zero
+    o_ref[taps + 1] = zero
+    o_ref[taps + 2] = zero
+
+    def body(k, carry):
+        w = w_ref[pl.ds(pl.multiple_of(k * gw, 16), gw), :]
+        lane = lane_of(w.shape)
+        o_ref[k + 1, 0:gw, :] = jnp.where(lane < gw, w, jnp.zeros_like(w))
+        o_ref[k + 1, gw : 2 * gw, :] = jnp.where(lane >= gw, w, jnp.zeros_like(w))
+        o_ref[k + 1, 2 * gw :, :] = jnp.zeros((LANES - 2 * gw, LANES), bf16)
+        return carry
+
+    lax.fori_loop(0, taps, body, 0)
+
+
+def phases_from_frames(x_ref, xf, ph, rows, frames, half):
+    blocks, block = x_ref.shape[0], x_ref.shape[2]
+    span = frames + 2 * half
+    for r in range(rows):
+        xf[r * span : r * span + half, :] = jnp.zeros((half, LANES), f32)
+        xf[r * span + half + frames : (r + 1) * span, :] = jnp.zeros((half, LANES), f32)
+        for s in range(blocks):
+            at = r * span + half + s * block
+            xf[at : at + block, :] = x_ref[s, r].astype(f32)
+    for p in range(16):
+        n = (span // 2) if p == 0 else (span // 2 - 16)
+        for r in range(rows):
+            for b in range(2):
+                ph[p, r, 0:n, b * LANES : (b + 1) * LANES] = xf[
+                    pl.ds(r * span + 2 * p + b, n, stride=2), :
+                ].astype(bf16)
+
+
+def window(ph, m, rows, n):
+    p, a = lax.rem(m, 16), m // 16
+    part = ph[p, :, pl.ds(pl.multiple_of(a * 16, 16), n), :]
+    return part.reshape(rows * n, part.shape[-1])
+
+
+def conv_kernel(rows, frames, half, c_ref, x_ref, w_ref, b_ref, pre_ref, keep_ref, send_ref, ph_ref, xf, acc):
+    n = frames // 2
+    phases_from_frames(x_ref, xf, ph_ref, rows, frames, half)
+    acc[...] = jnp.zeros_like(acc)
+
+    def body(i, carry):
+        total = None
+        for t in range(5):
+            m = i * 5 + t
+            here, before, after = w_ref[2 * m + 1], w_ref[2 * m], w_ref[2 * m + 2]
+            rhs = jnp.concatenate(
+                [jnp.concatenate([here, before], 1), jnp.concatenate([after, here], 1)], 0
+            )
+            part = dot_nn(window(ph_ref, m, rows, n), rhs)
+            total = part if total is None else total + part
+        acc[...] += total
+        return carry
+
+    lax.fori_loop(0, (half + 1) // 5, body, 0)
+    bias = jnp.concatenate([b_ref[...], b_ref[...]], 1)
+    c = c_ref[1]
+    for r in range(rows):
+        pre = acc[r * n : (r + 1) * n, :] + bias
+        pre_ref[r] = pre
+        x = ph_ref[0, r, half // 2 : half // 2 + n, :].astype(f32)
+        s = (x + gelu_and_slope(pre)[0]).astype(bf16)
+        for zf in range(4):
+            for xq in range(2):
+                for cf in range(2):
+                    u = ((zf * 2 + xq) * 2 + cf) * 16
+                    blk = s[u : u + 16, :]
+
+                    @pl.when(c == cf)
+                    def _(blk=blk, r=r, xq=xq, zf=zf):
+                        keep_ref[r, xq, zf * 16 : zf * 16 + 16, :] = blk
+
+                    @pl.when(c != cf)
+                    def _(blk=blk, r=r, xq=xq, zf=zf):
+                        send_ref[r, xq, zf * 16 : zf * 16 + 16, :] = blk
+
+
+def normed(values):
+    centre = jnp.mean(values, axis=-1, keepdims=True)
+    centred = values - centre
+    spread = jnp.mean(centred * centred, axis=-1, keepdims=True)
+    inverse = lax.rsqrt(spread + epsilon)
+    return centred * inverse, inverse
+
+
+def stem_norm_kernel(width, r_ref, g_ref, b_ref, h_ref, low_ref, n_ref, i_ref):
+    halves = []
+    for a in range(2):
+        pieces = [r_ref[j, :, a * LANES : (a + 1) * LANES].astype(f32) for j in range(r_ref.shape[0])]
+        halves.append(jnp.concatenate(tiles_of(pieces, width), axis=1))
+    s = jnp.concatenate(halves, axis=0)
+    n, inv = normed(s)
+    h = n * g_ref[0:1, :] + b_ref[1:2, :]
+    h_ref[...] = h
+    low_ref[...] = h.astype(bf16)
+    n_ref[...] = n
+    i_ref[...] = inv
+
+
+def attend_kernel(base, hl0, hl1, hl2, hl3, w_ref, m_ref, bq_ref, segr, segc,
+                  q_ref, k_ref, v_ref, at_ref, lse_ref, keep_ref, send_ref):
+    t = hl0.shape[0]
+    hl = jnp.concatenate([hl0[...], hl1[...], hl2[...], hl3[...]], axis=0)
+    proj = dot_nn(hl, w_ref[...])
+    q = ((proj[:, 0:256] + bq_ref[0:1, :]) * 0.125).astype(bf16)
+    k = proj[:, 256:512].astype(bf16)
+    v = (proj[:, 512:768] + bq_ref[1:2, :]).astype(bf16)
+    q_ref[...] = q
+    k_ref[...] = k
+    v_ref[...] = v
+    allowed = segc[...] == segr[...]
+    lane = lane_of((1, LANES))
+    parts = []
+    for head in range(3):
+        tile = head // 2
+        cols = slice(tile * LANES, (tile + 1) * LANES)
+        mine = (lane < 64) if head % 2 == 0 else (lane >= 64)
+        qh = jnp.where(mine, q[:, cols], jnp.zeros((), bf16))
+        s = dot_nt(qh, k[:, cols])
+        s = jnp.where(allowed, s, masked_score)
+        top = jnp.max(s, axis=-1, keepdims=True)
+        e = jnp.exp(s - top)
+        total = jnp.sum(e, axis=-1, keepdims=True)
+        lse_ref[head] = top + jnp.log(total)
+        p = (e * (1.0 / total)).astype(bf16)
+        parts.append(dot_nn(p, v[:, cols]))
+    att = jnp.concatenate([jnp.where(lane < 64, parts[0], parts[1]), parts[2]], axis=1).astype(bf16)
+    at_ref[...] = att
+    branch = dot_nn(att, m_ref[...]).astype(bf16)
+    for dx in range(2):
+        keep_ref[dx] = branch[2 * dx * t : (2 * dx + 1) * t]
+        send_ref[dx] = branch[(2 * dx + 1) * t : (2 * dx + 2) * t]
+
+
+def half_sum_kernel(a_ref, b_ref, own_ref, send_ref):
+    own_ref[...] = a_ref[0].astype(f32) + b_ref[0].astype(f32)
+    send_ref[...] = (a_ref[1].astype(f32) + b_ref[1].astype(f32)).astype(bf16)
+
+
+def norm_kernel(gain_row, bias_row, shift_row, h_ref, a_ref, r_ref, g_ref, b_ref, o_ref, low_ref, n_ref, i_ref):
+    v = h_ref[...] + (a_ref[...].astype(f32) + r_ref[...].astype(f32) + b_ref[bias_row : bias_row + 1, :])
+    n, inv = normed(v)
+    o = n * g_ref[gain_row : gain_row + 1, :] + b_ref[shift_row : shift_row + 1, :]
+    o_ref[...] = o
+    low_ref[...] = o.astype(bf16)
+    n_ref[...] = n
+    i_ref[...] = inv
+
+
+def feed_kernel(f0, f1, u0, u1, d0, d1, b_ref, act_ref, slope_ref, own_ref, send_ref):
+    t = f0.shape[0]
+    first = jnp.concatenate([f0[...], f1[...]], axis=0)
+    total = None
+    for i, (u, d) in enumerate(((u0, d0), (u1, d1))):
+        up = dot_nn(first, u[...]) + b_ref[i : i + 1, :]
+        act, slope = gelu_and_slope(up)
+        act = act.astype(bf16)
+        act_ref[i] = act
+        slope_ref[i] = slope.astype(bf16)
+        part = dot_nt(act, d[...])
+        total = part if total is None else total + part
+    own_ref[...] = total[:t]
+    send_ref[...] = total[t:].astype(bf16)
+
+
+def norm_back(g, n, inv, gain):
+    scaled = g * gain
+    m1 = jnp.mean(scaled, axis=-1, keepdims=True)
+    m2 = jnp.mean(scaled * n, axis=-1, keepdims=True)
+    return inv * (scaled - m1 - n * m2)
+
+
+def norm_sums(g, n, d, o_ref):
+    o_ref[0:1, :] = jnp.sum(g * n, axis=0, keepdims=True)
+    o_ref[1:2, :] = jnp.sum(g, axis=0, keepdims=True)
+    o_ref[2:3, :] = jnp.sum(d, axis=0, keepdims=True)
+    o_ref[3:8, :] = jnp.zeros((5, o_ref.shape[1]), f32)
+
+
+def norm_back_kernel(gain_row, count, *refs):
+    given, (g_ref, n_ref, i_ref, d_ref, low_ref, s_ref) = refs[:count], refs[count:]
+    g = given[0][...].astype(f32)
+    for r in given[1:]:
+        g = g + r[...].astype(f32)
+    n = n_ref[...]
+    d = norm_back(g, n, i_ref[...], g_ref[gain_row : gain_row + 1, :])
+    d_ref[...] = d
+    low_ref[...] = d.astype(bf16)
+    norm_sums(g, n, d, s_ref)
+
+
+def stem_norm_back_kernel(width, count, *refs):
+    given, (g_ref, n_ref, i_ref, o_ref, s_ref) = refs[:count], refs[count:]
+    g = given[0][...].astype(f32)
+    for r in given[1:]:
+        g = g + r[...].astype(f32)
+    n = n_ref[...]
+    d = norm_back(g, n, i_ref[...], g_ref[0:1, :])
+    norm_sums(g, n, d, s_ref)
+    t = d.shape[0] // 2
+    for a in range(2):
+        part = d[a * t : (a + 1) * t]
+        cols = [part[:, LANES * v : LANES * (v + 1)] for v in range(part.shape[1] // LANES)]
+        for j in range(o_ref.shape[0]):
+            o_ref[j, :, a * LANES : (a + 1) * LANES] = piece_of(cols, j, width).astype(bf16)
+
+
+def feed_back_kernel(e0, e1, u0, u1, d0, d1, slope_ref, dup_ref, own_ref, send_ref, bias_ref):
+    t = e0.shape[0]
+    d2 = jnp.concatenate([e0[...], e1[...]], axis=0)
+    total = None
+    for i, (u, d) in enumerate(((u0, d0), (u1, d1))):
+        dup = dot_nn(d2, d[...]) * slope_ref[i].astype(f32)
+        bias_ref[i : i + 1, :] = jnp.sum(dup, axis=0, keepdims=True)
+        dup = dup.astype(bf16)
+        dup_ref[i] = dup
+        part = dot_nt(dup, u[...])
+        total = part if total is None else total + part
+    bias_ref[2:8, :] = jnp.zeros((6, bias_ref.shape[1]), f32)
+    own_ref[...] = total[:t]
+    send_ref[...] = total[t:].astype(bf16)
+
+
+def feed_grad_kernel(place, f0, f1, e0, e1, act_ref, dup_ref, keep_ref, send_ref):
+    z, x = place[2], place[3]
+    width = keep_ref.shape[3]
+    first = jnp.concatenate([f0[...], f1[...]], axis=0)
+    d2 = jnp.concatenate([e0[...], e1[...]], axis=0)
+    for i, out in enumerate((keep_ref, send_ref)):
+        for kind, (a, b) in enumerate(((first, dup_ref[i]), (d2, act_ref[i]))):
+            g = dot_tn(a, b).astype(bf16)
+            for j in range(8):
+                zi, xi = j // 2, j % 2
+                out[zi ^ z, xi ^ x, kind] = g[j * width : (j + 1) * width]
+
+
+def attend_back_kernel(e0, e1, e2, e3, q_ref, k_ref, v_ref, lse_ref, w_ref, m_ref, segr, segc,
+                       dp_ref, dc_ref, keep_ref, send_ref, bias_ref):
+    t = e0.shape[0]
+    d1 = jnp.concatenate([e0[...], e1[...], e2[...], e3[...]], axis=0)
+    da = dot_nt(d1, m_ref[...]).astype(bf16)
+    q, k, v = q_ref[...], k_ref[...], v_ref[...]
+    allowed = segc[...] == segr[...]
+    lane = lane_of((1, LANES))
+    dq, dk, dv = [None] * 2, [None] * 2, [None] * 2
+    for head in range(3):
+        tile = head // 2
+        cols = slice(tile * LANES, (tile + 1) * LANES)
+        mine = (lane < 64) if head % 2 == 0 else (lane >= 64)
+        zero = jnp.zeros((), bf16)
+        qh = jnp.where(mine, q[:, cols], zero)
+        dah = jnp.where(mine, da[:, cols], zero)
+        s = dot_nt(qh, k[:, cols])
+        p = jnp.where(allowed, jnp.exp(s - lse_ref[head]), 0.0)
+        dp = dot_nt(dah, v[:, cols])
+        delta = jnp.sum(p * dp, axis=-1, keepdims=True)
+        ds = (p * (dp - delta)).astype(bf16)
+        a = dot_nn(ds, jnp.where(mine, k[:, cols], zero))
+        b = dot_tn(ds, qh)
+        c = dot_tn(p.astype(bf16), dah)
+        for held, new in ((dq, a), (dk, b), (dv, c)):
+            held[tile] = new if held[tile] is None else held[tile] + new
+    dq = [(d.astype(bf16) * jnp.array(0.125, bf16)).astype(f32) for d in dq]
+    dk = [d.astype(bf16).astype(f32) for d in dk]
+    dv = [d.astype(bf16).astype(f32) for d in dv]
+    wide = jnp.concatenate(dq + dk + dv, axis=1).astype(bf16)
+    dp_ref[...] = wide
+    bias_ref[0:1, :] = jnp.concatenate([jnp.sum(d, axis=0, keepdims=True) for d in dq], axis=1)
+    bias_ref[1:2, :] = jnp.concatenate([jnp.sum(d, axis=0, keepdims=True) for d in dv], axis=1)
+    bias_ref[2:8, :] = jnp.zeros((6, 256), f32)
+    k01 = pltpu.roll(dk[0], 64, 1)
+    dense = [dq[0], jnp.where(lane < 64, dq[1], k01), jnp.where(lane < 64, k01, pltpu.roll(dk[1], 64, 1)), dv[0], dv[1]]
+    dc_ref[...] = jnp.concatenate(dense, axis=1).astype(bf16)
+    out = dot_nt(wide, w_ref[...]).astype(bf16)
+    for dx in range(2):
+        keep_ref[dx] = out[2 * dx * t : (2 * dx + 1) * t]
+        send_ref[dx] = out[(2 * dx + 1) * t : (2 * dx + 2) * t]
+
+
+def attend_grad_kernel(place, hl0, hl1, hl2, hl3, e0, e1, e2, e3, at_ref, dc_ref, o_ref, m_ref):
+    z, x = place[2], place[3]
+    hl = jnp.concatenate([hl0[...], hl1[...], hl2[...], hl3[...]], axis=0)
+    d1 = jnp.concatenate([e0[...], e1[...], e2[...], e3[...]], axis=0)
+    g = dot_tn(hl, dc_ref[...]).astype(bf16)
+    width = o_ref.shape[2]
+    for j in range(8):
+        zi, xi = j // 2, j % 2
+        o_ref[zi ^ z, xi ^ x] = g[j * width : (j + 1) * width]
+    m_ref[...] = dot_tn(at_ref[...], d1)[0 : m_ref.shape[0]].astype(bf16)
+
+
+def stem_slope_kernel(rows, place, keep_ref, recv_ref, pre_ref, low_ref, ds_ref, bias_ref):
+    c = place[1]
+    for r in range(rows):
+        for zf in range(4):
+            for xq in range(2):
+                for rel, src in enumerate((keep_ref, recv_ref)):
+                    u = pl.multiple_of(((zf * 2 + xq) * 2 + (c ^ rel)) * 16, 16)
+                    ds_ref[r, pl.ds(u, 16), :] = src[r, xq, zf * 16 : zf * 16 + 16, :]
+    total = None
+    for r in range(rows):
+        dpre = ds_ref[r].astype(f32) * gelu_and_slope(pre_ref[r])[1]
+        part = jnp.sum(dpre, axis=0, keepdims=True)
+        total = part if total is None else total + part
+        low_ref[r] = dpre.astype(bf16)
+    bias_ref[0:1, :] = total[:, 0:LANES] + total[:, LANES : 2 * LANES]
+    bias_ref[1:8, :] = jnp.zeros((7, LANES), f32)
+
+
+def stem_grad_kernel(rows, taps, gw, place, ph_ref, low_ref, keep_ref, send_ref):
+    n = low_ref.shape[1]
+    y, c = place[0], place[1]
+    left = jnp.concatenate([low_ref[r] for r in range(rows)], axis=0).T
+    lane = lane_of((gw, LANES))
+    per = taps // 4
+    for rc, out in enumerate((keep_ref, send_ref)):
+        for ry in range(2):
+            block = (y ^ ry) * 2 + (c ^ rc)
+
+            def win(i):
+                at = pl.multiple_of((block + i // 16) * 16, 16)
+                return ph_ref[i % 16, :, pl.ds(at, n), :].reshape(rows * n, 2 * LANES)
+
+            def save(k, t, out=out, ry=ry):
+                out[ry, k * gw : (k + 1) * gw, :] = jnp.where(lane < gw, t[0:gw], t[gw : 2 * gw]).astype(bf16)
+
+            held = None
+            for i in range(per // 2 + 1):
+                if i < per // 2:
+                    g = dot_nn(left, win(i))
+                    cross = g[LANES:, 0:LANES]
+                else:
+                    cross = dot_nn(left[LANES:], win(i)[:, 0:LANES])
+                if held is not None:
+                    save(2 * i - 1, held + cross)
+                if i < per // 2:
+                    save(2 * i, g[0:LANES, 0:LANES] + g[LANES:, LANES:])
+                    held = g[0:LANES, LANES:]
+
+
+def stem_input_grad_kernel(rows, half, low_ref, ds_ref, w_ref, o_ref, qf, ph, acc):
+    n = low_ref.shape[1]
+    span = n + half
+    for r in range(rows):
+        qf[r, 0 : half // 2, :] = jnp.zeros((half // 2, 2 * LANES), f32)
+        qf[r, half // 2 + n :, :] = jnp.zeros((half // 2, 2 * LANES), f32)
+        qf[r, half // 2 : half // 2 + n, :] = low_ref[r].astype(f32)
+    for p in range(16):
+        m = span if p == 0 else span - 16
+        for r in range(rows):
+            ph[p, r, 0:m, :] = qf[r, p : p + m, :].astype(bf16)
+    acc[...] = jnp.zeros_like(acc)
+
+    def body(i, carry):
+        total = None
+        for t in range(5):
+            m = i * 5 + t
+            here, before, after = w_ref[2 * half + 1 - 2 * m], w_ref[2 * half - 2 * m], w_ref[2 * half + 2 - 2 * m]
+            rhs = jnp.concatenate(
+                [jnp.concatenate([here, before], 1), jnp.concatenate([after, here], 1)], 0
+            )
+            part = dot_nt(window(ph, m, rows, n), rhs)
+            total = part if total is None else total + part
+        acc[...] += total
+        return carry
+
+    lax.fori_loop(0, (half + 1) // 5, body, 0)
+    per = n // o_ref.shape[0]
+    for r in range(rows):
+        g = (acc[r * n : (r + 1) * n, :] + ds_ref[r].astype(f32)).astype(bf16)
+        for j in range(o_ref.shape[0]):
+            o_ref[j, r] = g[j * per : (j + 1) * per, :]
+
+
+def join_kernel(width, r_ref, o_ref, mixed):
+    blocks, rows, per = r_ref.shape[0], r_ref.shape[1], r_ref.shape[2]
+    for r in range(rows):
+        for a in range(2):
+            pieces = [r_ref[j, r, :, a * LANES : (a + 1) * LANES].astype(f32) for j in range(blocks)]
+            for v, col in enumerate(tiles_of(pieces, width)):
+                mixed[pl.ds(v * 2 * per + a, per, stride=2), :] = col
+        for v in range(o_ref.shape[2] // LANES):
+            o_ref[r, :, v * LANES : (v + 1) * LANES] = mixed[v * 2 * per : (v + 1) * 2 * per, :]
+
+
+def swapped(v, axis):
+    return lax.ppermute(v, axis, [(0, 1), (1, 0)])
+
+
+def across(v, axis, bit):
+    count = lax.axis_size(axis)
+    return lax.ppermute(v, axis, [(i, i ^ bit) for i in range(count)])
+
+
+def plus(a, b):
+    return (a.astype(f32) + b.astype(f32)).astype(bf16)
+
+
+def halved_z(v):
+    v = plus(v[0::2], across(v[1::2], "z", 1))
+    return plus(v[0], across(v[1], "z", 2))
+
+
+def local_rows(
+    features, cotangent, segments, stem_weight, projection_weight, mixing_weight,
+    feedforward_weight, norm_gains, biases, *state,
+):
+    rows, toks, width = features.shape
+    yi, ci, zi, xi = (lax.axis_index(a) for a in ("y", "c", "z", "x"))
+    place = jnp.stack([yi, ci, zi, xi]).astype(jnp.int32)
+    seq_i, row_i = zi * 2 + xi, yi * 2 + ci
+    seq = ("z", "x")
+    blocks = 8
+    share = width // blocks
+    gw = width // GROUPS
+    frames = toks * blocks
+    half = KERNEL // 2
+    layers = projection_weight.shape[0]
+    ff_rows = feedforward_weight.shape[3] // width
+    head_share = width // 4
+    group = 2 * xi + ci
+    t = rows * toks
+
+    stem_share = jnp.pad(
+        lax.dynamic_slice_in_dim(stem_weight, seq_i * share, share, 1), ((0, 0), (0, LANES - share))
+    )
+    taps = whole_call(
+        functools.partial(taps_kernel, KERNEL, gw), sds((KERNEL + 3, LANES, LANES), bf16), [stem_share]
+    )
+
+    def attend_weights(l):
+        parts = []
+        for i in range(3):
+            part = lax.dynamic_slice(
+                projection_weight, (l, 0, i * width + group * head_share), (1, width, head_share)
+            )[0]
+            parts.append(jnp.pad(part, ((0, 0), (0, 256 - head_share))))
+        mix = lax.dynamic_slice(mixing_weight, (l, group * head_share, 0), (1, head_share, width))[0]
+        base = 2 + l * (6 + ff_rows)
+        both = lax.dynamic_slice(biases, (base, group * head_share), (2, head_share))
+        return (
+            jnp.concatenate(parts, axis=1),
+            jnp.pad(mix, ((0, 256 - head_share), (0, 0))),
+            jnp.pad(both, ((0, 0), (0, 256 - head_share))),
+        )
+
+    def feed_weights(l):
+        ups, downs, ids = [], [], []
+        base = 2 + l * (6 + ff_rows)
+        for ry in range(2):
+            block = 2 * (yi ^ ry) + ci
+            part = lax.dynamic_slice(
+                feedforward_weight, (l, 0, 0, block * width), (1, width, 2, width)
+            )[0]
+            ups.append(part[:, 0, :])
+            downs.append(part[:, 1, :])
+            ids.append(lax.dynamic_slice_in_dim(biases, base + 6 + block, 1, 0))
+        return ups, downs, jnp.concatenate(ids, axis=0)
+
+    other = swapped(segments, "c")
+    four = jnp.where(ci == 0, jnp.concatenate([segments, other]), jnp.concatenate([other, segments]))
+    row_ids = lax.dynamic_index_in_dim(four, zi, 0, keepdims=False)
+    row_ids = row_ids.reshape(4, 2, 2, 16, 2).transpose(1, 2, 4, 0, 3)
+    row_ids = jnp.where(xi == 0, row_ids, row_ids[::-1])
+    row_ids = jnp.where(ci == 0, row_ids, row_ids[:, ::-1]).reshape(-1)
+    seg_row, seg_col = row_ids[None, :], row_ids[:, None]
+
+    sent = whole_call(
+        functools.partial(split_kernel, blocks, share), sds((blocks, rows, toks, LANES), bf16), [features]
+    )
+    mine = lax.all_to_all(sent, seq, 0, 0, tiled=True)
+    conv_bias = jnp.pad(
+        lax.dynamic_slice(biases, (0, seq_i * share), (1, share)), ((0, 0), (0, LANES - share))
+    )
+    n = frames // 2
+    exchange = sds((rows, 2, 64, 2 * LANES), bf16)
+    pre_act, kept, away, phases = whole_call(
+        functools.partial(conv_kernel, rows, frames, half),
+        [sds((rows, n, 2 * LANES), f32), exchange, exchange, sds((16, rows, (frames + 2 * half) // 2, 2 * LANES), bf16)],
+        [place, mine, taps, conv_bias],
+        scalars=1,
+        scratch=[pltpu.VMEM((rows * (frames + 2 * half), LANES), f32), pltpu.VMEM((rows * n, 2 * LANES), f32)],
+        flops=2 * rows * n * 256 * 256 * 65,
+    )
+    came = swapped(away, "c")
+    slots = jnp.where(ci == 0, jnp.concatenate([kept, came]), jnp.concatenate([came, kept]))
+    joined = lax.all_to_all(slots.reshape(blocks, 64, 2 * LANES), seq, 0, 0, tiled=True)
+    wide = sds((t, width), f32)
+    thin = sds((t, width), bf16)
+    column = sds((t, 1), f32)
+    hidden, hidden_low, normed_stem, inverse_stem = whole_call(
+        functools.partial(stem_norm_kernel, share), [wide, thin, wide, column], [joined, norm_gains, biases]
+    )
+
+    def gathered(v):
+        over_c = swapped(v, "c")
+        over_x = swapped(v, "x")
+        return [v, over_c, over_x, swapped(over_x, "c")]
+
+    def summed(keep, send):
+        own, pass_on = whole_call(half_sum_kernel, [wide, thin], [keep, swapped(send, "c")])
+        return own, swapped(pass_on, "x")
+
+    saved = []
+    two = sds((2, t, width), bf16)
+    full = 4 * t
+    for l in range(layers):
+        base = 2 + l * (6 + ff_rows)
+        in_w, mix_w, both_b = attend_weights(l)
+        ups, downs, up_b = feed_weights(l)
+        hl = gathered(hidden_low)
+        q, k, v, att, lse, keep, send = whole_call(
+            functools.partial(attend_kernel, base),
+            [sds((full, 256), bf16)] * 4 + [sds((3, full, 1), f32), two, two],
+            hl + [in_w, mix_w, both_b, seg_row, seg_col],
+            flops=2 * full * (768 * 768 + 256 * 768 + 3 * full * 256),
+        )
+        own, rest = summed(keep, send)
+        first, first_low, n1, i1 = whole_call(
+            functools.partial(norm_kernel, 1 + 2 * l, base + 2, base + 3),
+            [wide, thin, wide, column],
+            [hidden, own, rest, norm_gains, biases],
+        )
+        first_other = swapped(first_low, "c")
+        act, slope, own, send = whole_call(
+            feed_kernel,
+            [sds((2, 2 * t, width), bf16)] * 2 + [wide, thin],
+            [first_low, first_other, *ups, *downs, up_b],
+            flops=2 * 2 * t * width * width * 4,
+        )
+        hidden, hidden_low, n2, i2 = whole_call(
+            functools.partial(norm_kernel, 2 + 2 * l, base + 4, base + 5),
+            [wide, thin, wide, column],
+            [first, own, swapped(send, "c"), norm_gains, biases],
+        )
+        saved.append((in_w, mix_w, ups, downs, hl, q, k, v, att, lse, n1, i1, first_low, first_other, act, slope, n2, i2))
+
+    by_z = hidden.astype(bf16).reshape(2, 4, 16, width).transpose(1, 2, 0, 3).reshape(4, 32, width)
+    by_z = lax.all_to_all(by_z, "z", 0, 0, tiled=True).reshape(2, 2, 32, width)
+    stay = lax.dynamic_index_in_dim(by_z, ci, 0, keepdims=False)
+    move = swapped(lax.dynamic_index_in_dim(by_z, 1 - ci, 0, keepdims=False), "c")
+    encoded = jnp.where(ci == 0, jnp.stack([stay, move], 1), jnp.stack([move, stay], 1))
+    encoded = encoded.reshape(rows, toks, width).astype(f32)
+
+    cot = cotangent.reshape(rows, 2, 16, 2, width).transpose(1, 0, 3, 2, 4)
+    stay = lax.dynamic_index_in_dim(cot, ci, 0, keepdims=False)
+    move = swapped(lax.dynamic_index_in_dim(cot, 1 - ci, 0, keepdims=False), "c")
+    cot = jnp.where(ci == 0, jnp.concatenate([stay, move]), jnp.concatenate([move, stay]))
+    cot = lax.all_to_all(cot, "z", 0, 0, tiled=True)
+    cot = cot.transpose(1, 0, 2, 3).reshape(t, width)
+
+    sums = sds((8, width), f32)
+    terms = [cot]
+    gain_grads = [None] * norm_gains.shape[0]
+    bias_grads = [None] * biases.shape[0]
+    feed_grads, in_grads, mix_grads = [None] * layers, [None] * layers, [None] * layers
+    part_shape = sds((4, 2, 2, share, width), bf16)
+    for l in reversed(range(layers)):
+        base = 2 + l * (6 + ff_rows)
+        in_w, mix_w, ups, downs, hl, q, k, v, att, lse, n1, i1, first_low, first_other, act, slope, n2, i2 = saved[l]
+        d2, d2_low, small = whole_call(
+            functools.partial(norm_back_kernel, 2 + 2 * l, len(terms)), [wide, thin, sums], terms + [norm_gains, n2, i2]
+        )
+        gain_grads[2 + 2 * l], bias_grads[base + 5], bias_grads[base + 4] = small[0], small[1], small[2]
+        d2_other = swapped(d2_low, "c")
+        dup, own, send, up_sums = whole_call(
+            feed_back_kernel,
+            [sds((2, 2 * t, width), bf16), wide, thin, sums],
+            [d2_low, d2_other, *ups, *downs, slope],
+            flops=2 * 2 * t * width * width * 4,
+        )
+        zero_row = jnp.zeros((ff_rows, width), f32)
+        for ry in range(2):
+            zero_row = lax.dynamic_update_slice_in_dim(zero_row, up_sums[ry : ry + 1], 2 * (yi ^ ry) + ci, 0)
+        for i in range(ff_rows):
+            bias_grads[base + 6 + i] = zero_row[i]
+        d1, d1_low, small = whole_call(
+            functools.partial(norm_back_kernel, 1 + 2 * l, 3),
+            [wide, thin, sums],
+            [d2, own, swapped(send, "c"), norm_gains, n1, i1],
+        )
+        gain_grads[1 + 2 * l], bias_grads[base + 3], bias_grads[base + 2] = small[0], small[1], small[2]
+        dl = gathered(d1_low)
+        keep, send = whole_call(
+            feed_grad_kernel,
+            [part_shape, part_shape],
+            [place, first_low, first_other, d2_low, d2_other, act, dup],
+            scalars=1,
+            flops=2 * 2 * t * width * width * 4,
+        )
+        part = plus(keep, swapped(send, "y"))
+        part = halved_z(part)
+        feed_grads[l] = plus(part[0], swapped(part[1], "x"))
+        wide_dp, dense_dp, keep, send, small = whole_call(
+            attend_back_kernel,
+            [sds((full, 768), bf16), sds((full, 640), bf16), two, two, sds((8, 256), f32)],
+            dl + [q, k, v, lse, in_w, mix_w, seg_row, seg_col],
+            flops=2 * full * (768 * 768 + 256 * 768 + 3 * full * 640),
+        )
+        for i in range(2):
+            bias_grads[base + i] = lax.dynamic_update_slice_in_dim(
+                jnp.zeros((width,), f32), small[i, :head_share], group * head_share, 0
+            )
+        own, rest = summed(keep, send)
+        terms = [d1, own, rest]
+        in_part, mix_part = whole_call(
+            attend_grad_kernel,
+            [sds((4, 2, share, 640), bf16), sds((head_share, width), bf16)],
+            [place] + hl + dl + [att, dense_dp],
+            scalars=1,
+            flops=2 * full * width * (640 + 256),
+        )
+        part = halved_z(in_part)
+        mine_cols, other_cols = part[0, :, : 3 * head_share], swapped(part[1], "x")[:, : 3 * head_share]
+        low_g = jnp.where(xi == 0, mine_cols, other_cols).reshape(share, 3, head_share)
+        high_g = jnp.where(xi == 0, other_cols, mine_cols).reshape(share, 3, head_share)
+        upper = jnp.stack([low_g[:, 0], high_g[:, 0], low_g[:, 1]])
+        lower = jnp.stack([high_g[:, 1], low_g[:, 2], high_g[:, 2]])
+        stay = jnp.where(yi == 0, upper, lower)
+        move = swapped(jnp.where(yi == 0, lower, upper), "y")
+        part = plus(stay, move)
+        swap_in = swapped(jnp.where(ci == 0, part[2], part[0]), "c")
+        first_block = jnp.where(ci == 0, part[0], part[1])
+        last_block = jnp.where(ci == 0, part[1], part[2])
+        in_grads[l] = jnp.concatenate([first_block, swap_in, last_block], axis=1).astype(f32)
+        part = mix_part.reshape(2, share, 2, 2, head_share).transpose(2, 0, 3, 1, 4)
+        stay = lax.dynamic_index_in_dim(part, yi, 0, keepdims=False)
+        move = swapped(lax.dynamic_index_in_dim(part, 1 - yi, 0, keepdims=False), "y")
+        part = plus(stay, move).reshape(4, share, head_share)
+        lane0 = jnp.where((zi & 1) == 0, part, part.reshape(2, 2, share, head_share)[:, ::-1].reshape(part.shape))
+        part = jnp.where((zi & 2) == 0, lane0, lane0.reshape(2, 2, share, head_share)[::-1].reshape(part.shape))
+        part = halved_z(part)
+        route = []
+        for c in range(2):
+            for z in range(4):
+                for x in range(2):
+                    route.append(((c * 4 + z) * 2 + x, ((z & 1) * 4 + (2 * x + c)) * 2 + (z >> 1)))
+        mix_grads[l] = lax.ppermute(part, ("c", "z", "x"), route).astype(f32)
+
+    ds_sent, small = whole_call(
+        functools.partial(stem_norm_back_kernel, share, len(terms)),
+        [sds((blocks, 64, 2 * LANES), bf16), sums],
+        terms + [norm_gains, normed_stem, inverse_stem],
+    )
+    gain_grads[0], bias_grads[1] = small[0], small[1]
+    bias_grads[0] = jnp.zeros((width,), f32)
+    slots = lax.all_to_all(ds_sent, seq, 0, 0, tiled=True).reshape(2, 2, 2, 64, 2 * LANES)
+    stay = lax.dynamic_index_in_dim(slots, ci, 0, keepdims=False)
+    move = swapped(lax.dynamic_index_in_dim(slots, 1 - ci, 0, keepdims=False), "c")
+    pair = sds((rows, n, 2 * LANES), bf16)
+    dpre_low, ds, stem_sums = whole_call(
+        functools.partial(stem_slope_kernel, rows), [pair, pair, sds((8, LANES), f32)],
+        [place, stay, move, pre_act], scalars=1,
+    )
+    quarter = sds((2, KERNEL // 4 * gw, LANES), bf16)
+    keep, send = whole_call(
+        functools.partial(stem_grad_kernel, rows, KERNEL, gw), [quarter, quarter], [place, phases, dpre_low],
+        scalars=1, flops=2 * rows * n * 256 * 256 * 65,
+    )
+    part = plus(keep, swapped(send, "c"))
+    stem_grad = plus(part[0], swapped(part[1], "y"))[:, : 2 * gw].astype(f32)
+    stem_grad = stem_grad.reshape(KERNEL // 4, gw, 2, gw).transpose(0, 3, 2, 1).reshape(KERNEL // 4 * gw, 2 * gw)
+    back = whole_call(
+        functools.partial(stem_input_grad_kernel, rows, half),
+        sds((blocks, rows, toks // 2, 2 * LANES), bf16),
+        [dpre_low, ds, taps],
+        scratch=[
+            pltpu.VMEM((rows, n + half, 2 * LANES), f32),
+            pltpu.VMEM((16, rows, n + half, 2 * LANES), bf16),
+            pltpu.VMEM((rows * n, 2 * LANES), f32),
+        ],
+        flops=2 * rows * n * 256 * 256 * 65,
+    )
+    back = lax.all_to_all(back, seq, 0, 0, tiled=True)
+    features_gradient = whole_call(
+        functools.partial(join_kernel, share), sds((rows, toks, width), f32), [back],
+        scratch=[pltpu.VMEM((width // LANES * toks, LANES), f32)],
+    )
+
+    smalls = jnp.stack(gain_grads + bias_grads)
+    smalls = smalls.reshape(smalls.shape[0], blocks, share).transpose(1, 0, 2)
+    smalls = jnp.sum(lax.all_to_all(smalls, seq, 0, 0, tiled=True), axis=0)
+    gain_count = norm_gains.shape[0]
+    smalls = smalls.at[gain_count].add(stem_sums[0, :share])
+    smalls = smalls + swapped(smalls, "c")
+    smalls = smalls + swapped(smalls, "y")
+
+    totals = (
+        stem_grad,
+        jnp.stack(in_grads),
+        jnp.stack(mix_grads),
+        jnp.stack(feed_grads).transpose(0, 2, 1, 3).astype(f32),
+        smalls[:gain_count],
+        smalls[gain_count:],
+    )
+    rate_base = 1.0 / math.sqrt(rows * 4 * frames)
+    olds = (stem_weight, projection_weight, mixing_weight, feedforward_weight, norm_gains, biases)
+    return (encoded, features_gradient, *updates(totals, olds, state, seq_i, row_i, 8, 4, rate_base))
+
+
+def updates(totals, olds, state, seq_index, row_index, seq_count, row_total, rate_base):
+    momenta, averaged, updated = [], [], []
+    for param_index in range(6):
+        old_share = olds[param_index]
+        share_width = old_share.shape[1] // seq_count
+        old_share = lax.dynamic_slice_in_dim(old_share, seq_index * share_width, share_width, 1)
+        if param_index < 4:
+            split_dim = row_dims[param_index]
+            piece_size = old_share.shape[split_dim] // row_total
+            old_share = lax.dynamic_slice_in_dim(
+                old_share, row_index * piece_size, piece_size, split_dim
+            )
+        old_share = old_share.astype(jnp.float32)
+        moment_new = momentum_decay * state[param_index] + totals[param_index]
+        weight_new = old_share - rate_factors[param_index] * rate_base * (
+            totals[param_index] + momentum_decay * moment_new
+        )
+        momenta.append(moment_new)
+        updated.append(weight_new)
+        averaged.append(
+            average_decay * state[6 + param_index] + (1.0 - average_decay) * weight_new
+        )
+    return (*momenta, *averaged, *updated)
+
+
 def solution(mesh):
+    if mesh.shape["row"] == 4 and mesh.shape["seq"] == 8:
+        body, mesh = local_rows, Mesh(mesh.devices.reshape(2, 2, 4, 2), ("y", "c", "z", "x"))
+        row, seq = ("y", "c"), ("z", "x")
+    else:
+        body, row, seq = local, "row", "seq"
     in_specs = (
-        P("row", "seq", None),
-        P("row", "seq", None),
-        P("row", None),
+        P(row, seq, None),
+        P(row, seq, None),
+        P(row, None),
         P(),
         P(),
         P(),
         P(),
         P(),
         P(),
-        P("row", "seq"),
-        P(None, "seq", "row"),
-        P(None, "seq", "row"),
-        P(None, "seq", None, "row"),
-        P(None, "seq"),
-        P(None, "seq"),
-        P("row", "seq"),
-        P(None, "seq", "row"),
-        P(None, "seq", "row"),
-        P(None, "seq", None, "row"),
-        P(None, "seq"),
-        P(None, "seq"),
+        P(row, seq),
+        P(None, seq, row),
+        P(None, seq, row),
+        P(None, seq, None, row),
+        P(None, seq),
+        P(None, seq),
+        P(row, seq),
+        P(None, seq, row),
+        P(None, seq, row),
+        P(None, seq, None, row),
+        P(None, seq),
+        P(None, seq),
     )
     out_specs = (
-        P("row", "seq", None),
-        P("row", "seq", None),
-        P("row", "seq"),
-        P(None, "seq", "row"),
-        P(None, "seq", "row"),
-        P(None, "seq", None, "row"),
-        P(None, "seq"),
-        P(None, "seq"),
-        P("row", "seq"),
-        P(None, "seq", "row"),
-        P(None, "seq", "row"),
-        P(None, "seq", None, "row"),
-        P(None, "seq"),
-        P(None, "seq"),
-        P("row", "seq"),
-        P(None, "seq", "row"),
-        P(None, "seq", "row"),
-        P(None, "seq", None, "row"),
-        P(None, "seq"),
-        P(None, "seq"),
-    )
-    return jax.shard_map(local, mesh=mesh, in_specs=in_specs, out_specs=out_specs, check_vma=False)
+        P(row, seq, None),
+        P(row, seq, None),
+        P(row, seq),
+        P(None, seq, row),
+        P(None, seq, row),
+        P(None, seq, None, row),
+        P(None, seq),
+        P(None, seq),
+        P(row, seq),
+        P(None, seq, row),
+        P(None, seq, row),
+        P(None, seq, None, row),
+        P(None, seq),
+        P(None, seq),
+        P(row, seq),
+        P(None, seq, row),
+        P(None, seq, row),
+        P(None, seq, None, row),
+        P(None, seq),
+        P(None, seq),
+    )
+    return jax.shard_map(body, mesh=mesh, in_specs=in_specs, out_specs=out_specs, check_vma=False)

time: 2140 us -> 560 us (0.26)
  waiting for transfers between devices: 1220 us -> 171 us
  local copies, waits for them, and re-layouts: 479 us -> 156 us
  matrix products: 269 us -> 0 us
  starting transfers between devices: 13.5 us -> 109 us
  Pallas kernels: 0 us -> 85.8 us
  other arithmetic: 110 us -> 32.4 us
    reduce_scatter x7 -> x0, waiting for transfers between devices: 827 us -> none  [the longest x1 515 us: local(): lax.psum_scatter(layer_partials[2], 'seq', scatter_dimension=1, tiled=True)]
    unnamed x19 -> x0, waiting for transfers between devices: 312 us -> none
    rev x2, local copies, waits for them, and re-layouts: 174 us -> 4.76 us  [local_rows(): part.reshape(2, 2, share, head_share)[:, ::-1].reshape(part.shape)]
    ppermute x4 -> x63, waiting for transfers between devices: 0.01 us -> 151 us  [the longest x12 76.9 us: across(): return lax.ppermute(v, axis, [(i, i ^ bit) for i in range(count)])]
    conv_general_dilated x3 -> x0, matrix products: 146 us -> none  [the longest x1 74.7 us: group_conv_kernel_grad(): lax.conv_general_dilated(extended, upstream_low, (1,), 'VALID', dimension...]
    dot_general x38 -> x0, matrix products: 123 us -> none  [the longest x2 15.7 us: local(): jnp.einsum('rtd,dj->rtj', down_low, down_matrix, preferred_element_type=j...]
    pallas_call x0 -> x33, Pallas kernels: none -> 85.8 us  [whole_call(): pl.pallas_call(kernel, out_shape=list(outs) if many else outs, in_specs=i...]
    all_gather x2 -> x0, waiting for transfers between devices: 78.3 us -> none  [local(): kv_whole = lax.all_gather(kv_local, 'seq', axis=1, tiled=True)]
  transfers between devices with their start and end apart: 18 -> 70, of which waited for: 9 -> 27; matrix products, arithmetic and copies ran while one was open for 31% -> 23% of each run, Pallas kernels for 0% -> 13%
where the time goes in v1:
time: 560 us; the launch traced here: 557 us
  waiting for transfers between devices  171 us (31%)
  local copies, waits for them, and re-layouts  156 us (28%)
  starting transfers between devices  109 us (19%)
  Pallas kernels  85.8 us (15%)
  other arithmetic  32.4 us (6%)
    pallas_call x33, Pallas kernels, whole_call(): pl.pallas_call(kernel, out_shape=list(outs) if many else outs, in_specs=i...  85.8 us
    ppermute x12, waiting for transfers between devices, across(): return lax.ppermute(v, axis, [(i, i ^ bit) for i in range(count)])  76.9 us
    unnamed x381, local copies, waits for them, and re-layouts  75.5 us
    ppermute x49, waiting for transfers between devices, swapped(): return lax.ppermute(v, axis, [(0, 1), (1, 0)])  73.6 us
    ppermute x49, starting transfers between devices, swapped(): return lax.ppermute(v, axis, [(0, 1), (1, 0)])  51.6 us
    ppermute x12, starting transfers between devices, across(): return lax.ppermute(v, axis, [(i, i ^ bit) for i in range(count)])  20.7 us
    convert_element_type x19, other arithmetic, plus(): return (a.astype(f32) + b.astype(f32)).astype(bf16)  17.2 us
    all_to_all x1, waiting for transfers between devices, local_rows(): lax.all_to_all(ds_sent, seq, 0, 0, tiled=True)  13.4 us
  transfers between devices with their start and end apart: 70, of which 27 were waited for; matrix products, arithmetic and copies ran while one was open for 23% of the time, Pallas kernels for 13%

profile of v1, /device:TPU:0, one launch (start us, length us, event | category | flops | bytes accessed | tf_op | source)
XLA Modules:
  0.0 557.0 jit_solution(11379416648536623368)
XLA Ops:
  2.4 7.3 %all-to-all-start = ((bf16[8,2,64,128]{3,2,1,0:T(8,128)(2,1)}), bf16[8,2,64,128]{3,2,1,0:T(8,128)(2,1)S(1)}, u32[]{:S(2)}, u32[]{:S(2)}) async-start(bf16[8,2,64,128]{3,2,1,0:T(8,128)(2,1)} %shard_map.356), calls=%async_computation | async-start | bytes 524288 | tf_op jit(solution)/shard_map/all_to_all | solution.py:1121
  9.7 11.0 %constant_dynamic-slice_fusion.8 = (bf16[1,768,2,768]{3,2,1,0:T(2,128)(2,1)}, bf16[1,768,2,768]{3,2,1,0:T(2,128)(2,1)}, bf16[1,768,2,768]{3,2,1,0:T(2,128)(2,1)}, bf16[1,768,2,768]{3,2,1,0:T(2,128)(2,1)}) fusion(bf16[2,768,2,3072]{3,2,1,0:T(2,128)(2,1)} %param.29, s32[]{:T(128)S(6)} %select_n.285, s32[]{:T(128)S(6)} %select_n.284), kind=kLoop, calls=%fused_computation.173 | loop fusion | bytes 18874376 | tf_op jit(solution)/shard_map/dynamic_slice | solution.py:1102
  29.3 10.8 %shard_map.358 = (f32[2,256,256]{2,1,0:T(8,128)S(1)}, bf16[2,2,64,256]{3,2,1,0:T(8,128)(2,1)S(1)}, bf16[2,2,64,256]{3,2,1,0:T(8,128)(2,1)S(1)}, bf16[16,2,320,256]{3,2,1,0:T(8,128)(2,1)}) custom-call(s32[4]{0:T(128)S(1)} %pad_add_fusion.c_ref.place, bf16[8,2,64,128]{3,2,1,0:T(8,128)(2,1)S(1)} %all-to-all-done.x_ref, bf16[131,128,128]{2,1,0:T(8,128)(2,1)S(1)} %copy-done.7, ...), custom_call_target="tpu_custom_call" | custom-call | flops 4362076160 | bytes 10584592 | tf_op jit(solution)/shard_map/pallas_call | solution.py:567
  40.6 4.2 dynamic-slice_bitcast_fusion.2
  45.5 5.7 %all-to-all-start.1 = ((bf16[8,64,256]{2,1,0:T(8,128)(2,1)}), bf16[8,64,256]{2,1,0:T(8,128)(2,1)S(1)}, u32[]{:S(2)}, u32[]{:S(2)}) async-start(bf16[8,64,256]{2,1,0:T(8,128)(2,1)} %bitcast.4), calls=%async_computation.1 | async-start | bytes 524288 | tf_op jit(solution)/shard_map/all_to_all | solution.py:1137
  54.3 5.9 %all-to-all-done.1.r_ref = bf16[8,64,256]{2,1,0:T(8,128)(2,1)S(1)} async-done(((bf16[8,64,256]{2,1,0:T(8,128)(2,1)}), bf16[8,64,256]{2,1,0:T(8,128)(2,1)S(1)}, u32[]{:S(2)}, u32[]{:S(2)}) %all-to-all-start.1) | async-done | bytes 262176 | tf_op jit(solution)/shard_map/all_to_all | solution.py:1137
  64.2 4.2 collective-permute-done.2.hl2
  76.2 4.5 copy_bitcast_fusion.2
  85.4 5.6 %collective-permute-done.6.r_ref = bf16[128,768]{1,0:T(8,128)(2,1)S(1)} collective-permute-done((bf16[128,768]{1,0:T(8,128)(2,1)S(1)}, bf16[128,768]{1,0:T(8,128)(2,1)S(1)}, u32[]{:S(2)}, u32[]{:S(2)}) %collective-permute-start.6) | collective-permute-done | bytes 196640 | tf_op jit(solution)/shard_map/ppermute | solution.py:1037
  120.5 4.3 collective-permute-done.13.r_ref
  127.8 13.0 %collective-permute-start.14 = (bf16[128,768]{1,0:T(8,128)(2,1)}, bf16[128,768]{1,0:T(8,128)(2,1)}, u32[]{:S(2)}, u32[]{:S(2)}) collective-permute-start(bf16[128,768]{1,0:T(8,128)(2,1)} %get-tuple-element.147.f0), channel_id=1, source_target_pairs={{0,8},{8,0},{1,9},{9,1},{2,10},{10,2},{3,11},{11,3},{4,12},{12,4},... | collective-permute-start | bytes 589832 | tf_op jit(solution)/shard_map/ppermute | solution.py:1037
  183.8 4.8 all-to-all-start.2
  204.1 4.1 collective-permute-done.21.e2
  210.5 4.2 shard_map.388
  228.8 6.0 %shard_map.373 = (bf16[512,768]{1,0:T(8,128)(2,1)}, bf16[512,640]{1,0:T(8,128)(2,1)S(1)}, bf16[2,128,768]{2,1,0:T(8,128)(2,1)S(1)}, bf16[2,128,768]{2,1,0:T(8,128)(2,1)S(1)}, f32[8,256]{1,0:T(8,128)S(1)}) custom-call(bf16[128,768]{1,0:T(8,128)(2,1)} %get-tuple-element.161.e0, bf16[128,768]{1,0:T(8,128)(2,1)} %collective-permute-done.20.e1, ...), custom_call_target="tpu_custom_call" | custom-call | flops 1811939328 | bytes 5392384 | tf_op jit(solution)/shard_map/pallas_call | solution.py:567
  248.1 26.2 %collective-permute-done.49 = bf16[2,2,96,192]{3,1,2,0:T(2,128)(2,1)S(1)} collective-permute-done((bf16[2,2,96,192]{3,1,2,0:T(2,128)(2,1)S(1)}, bf16[2,2,96,192]{3,1,2,0:T(2,128)(2,1)S(1)}, u32[]{:S(2)}, u32[]{:S(2)}) %collective-permute-start.49) | collective-permute-done | bytes 147488 | tf_op jit(solution)/shard_map/ppermute | solution.py:1037
  300.8 7.9 %collective-permute-done.41 = bf16[2,96,640]{2,1,0:T(8,128)(2,1)S(1)} collective-permute-done((bf16[2,96,640]{2,1,0:T(8,128)(2,1)S(1)}, bf16[2,96,640]{2,1,0:T(8,128)(2,1)S(1)}, u32[]{:S(2)}, u32[]{:S(2)}) %collective-permute-start.41) | collective-permute-done | bytes 245792 | tf_op jit(solution)/shard_map/ppermute | solution.py:1042
  330.1 5.7 %shard_map.378 = (bf16[512,768]{1,0:T(8,128)(2,1)}, bf16[512,640]{1,0:T(8,128)(2,1)S(1)}, bf16[2,128,768]{2,1,0:T(8,128)(2,1)S(1)}, bf16[2,128,768]{2,1,0:T(8,128)(2,1)S(1)}, f32[8,256]{1,0:T(8,128)S(1)}) custom-call(bf16[128,768]{1,0:T(8,128)(2,1)S(1)} %get-tuple-element.180.e0, bf16[128,768]{1,0:T(8,128)(2,1)S(1)} %collective-permute-done.27.e1, ...), custom_call_target="tpu_custom_call" | custom-call | flops 1811939328 | bytes 5392384 | tf_op jit(solution)/shard_map/pallas_call | solution.py:567
  339.1 5.9 %collective-permute-done.45 = bf16[2,2,96,192]{3,1,2,0:T(2,128)(2,1)S(1)} collective-permute-done((bf16[2,2,96,192]{3,1,2,0:T(2,128)(2,1)S(1)}, bf16[2,2,96,192]{3,1,2,0:T(2,128)(2,1)S(1)}, u32[]{:S(2)}, u32[]{:S(2)}) %collective-permute-start.45) | collective-permute-done | bytes 147488 | tf_op jit(solution)/shard_map/ppermute | solution.py:1037
  352.6 10.2 %collective-permute-done.47 = bf16[96,192]{1,0:T(8,128)(2,1)} collective-permute-done((bf16[96,192]{1,0:T(8,128)(2,1)S(1)}, bf16[96,192]{1,0:T(8,128)(2,1)}, u32[]{:S(2)}, u32[]{:S(2)}) %collective-permute-start.47) | collective-permute-done | bytes 36896 | tf_op jit(solution)/shard_map/ppermute | solution.py:1042
  365.3 6.3 %collective-permute-start.31 = (bf16[128,768]{1,0:T(8,128)(2,1)S(1)}, bf16[128,768]{1,0:T(8,128)(2,1)S(1)}, u32[]{:S(2)}, u32[]{:S(2)}) collective-permute-start(bf16[128,768]{1,0:T(8,128)(2,1)S(1)} %get-tuple-element.188), channel_id=1, source_target_pairs={{0,1},{1,0},{2,3},{3,2},{4,5},{5,4},{6,7},{7,6},{8,9},{9,8},{10,11... | collective-permute-start | bytes 589832 | tf_op jit(solution)/shard_map/ppermute | solution.py:1037
  371.6 4.2 collective-permute-start.36
  379.0 5.4 collective-permute-done.36
  401.3 4.6 all-to-all-start.4
  405.9 13.1 %collective-permute-done.38 = bf16[3,96,192]{1,2,0:T(8,128)(2,1)S(1)} collective-permute-done((bf16[3,96,192]{1,2,0:T(8,128)(2,1)S(1)}, bf16[3,96,192]{1,2,0:T(8,128)(2,1)S(1)}, u32[]{:S(2)}, u32[]{:S(2)}) %collective-permute-start.38) | collective-permute-done | bytes 110624 | tf_op jit(solution)/shard_map/ppermute | solution.py:1037
  419.3 13.4 %all-to-all-done.4 = bf16[8,64,256]{2,1,0:T(8,128)(2,1)S(1)} async-done(((bf16[8,64,256]{2,1,0:T(8,128)(2,1)}), bf16[8,64,256]{2,1,0:T(8,128)(2,1)S(1)}, u32[]{:S(2)}, u32[]{:S(2)}) %all-to-all-start.4) | async-done | bytes 262176 | tf_op jit(solution)/shard_map/all_to_all | solution.py:1297
  439.6 8.4 %shard_map.384 = (bf16[2,1536,128]{2,1,0:T(8,128)(2,1)S(1)}, bf16[2,1536,128]{2,1,0:T(8,128)(2,1)}) custom-call(s32[4]{0:T(128)S(1)} %pad_add_fusion.c_ref.place, bf16[16,2,320,256]{3,2,1,0:T(8,128)(2,1)} %get-tuple-element.195.ph_ref, bf16[2,256,256]{2,1,0:T(8,128)(2,1)S(1)} %get-tuple-element.193.low_ref), custom_call_target="tpu_custom_call" | custom-call | flops 4362076160 | bytes 7077904 | tf_op jit(solution)/shard_map/pallas_call | solution.py:567
  448.6 9.1 %shard_map.382 = bf16[8,2,32,256]{3,2,1,0:T(8,128)(2,1)} custom-call(bf16[2,256,256]{2,1,0:T(8,128)(2,1)S(1)} %get-tuple-element.193.low_ref, bf16[2,256,256]{2,1,0:T(8,128)(2,1)S(1)} %get-tuple-element.194.ds_ref, bf16[131,128,128]{2,1,0:T(8,128)(2,1)S(1)} %bitcast.243), custom_call_target="tpu_custom_call" | custom-call | flops 4362076160 | bytes 5079040 | tf_op jit(solution)/shard_map/pallas_call | solution.py:567
  478.4 17.9 %collective-permute-done.59 = bf16[2,2,96,768]{3,2,1,0:T(8,128)(2,1)} collective-permute-done((bf16[2,2,96,768]{3,2,1,0:T(8,128)(2,1)}, bf16[2,2,96,768]{3,2,1,0:T(8,128)(2,1)}, u32[]{:S(2)}, u32[]{:S(2)}) %collective-permute-start.59) | collective-permute-done | bytes 589856 | tf_op jit(solution)/shard_map/ppermute | solution.py:1042
  497.5 15.0 %collective-permute-done.54 = bf16[2,2,2,96,768]{4,3,2,1,0:T(8,128)(2,1)S(1)} collective-permute-done((bf16[2,2,2,96,768]{4,3,2,1,0:T(8,128)(2,1)S(1)}, bf16[2,2,2,96,768]{4,3,2,1,0:T(8,128)(2,1)S(1)}, u32[]{:S(2)}, u32[]{:S(2)}) %collective-permute-start.54) | collective-permute-done | bytes 1179680 | tf_op jit(solution)/shard_map/ppermute | solution.py:1042
  523.1 18.6 %collective-permute-done.55 = bf16[2,2,96,768]{3,2,1,0:T(8,128)(2,1)} collective-permute-done((bf16[2,2,96,768]{3,2,1,0:T(8,128)(2,1)}, bf16[2,2,96,768]{3,2,1,0:T(8,128)(2,1)}, u32[]{:S(2)}, u32[]{:S(2)}) %collective-permute-start.55) | collective-permute-done | bytes 589856 | tf_op jit(solution)/shard_map/ppermute | solution.py:1042
  546.3 4.2 collective-permute-done.56
  (676 shorter events, 282.3 us)
Async XLA Ops:
  2.4 24.6 %all-to-all-start = ((bf16[8,2,64,128]{3,2,1,0:T(8,128)(2,1)}), bf16[8,2,64,128]{3,2,1,0:T(8,128)(2,1)S(1)}, u32[]{:S(2)}, u32[]{:S(2)}) async-start(bf16[8,2,64,128]{3,2,1,0:T(8,128)(2,1)} %shard_map.356), calls=%async_computation | async-start | bytes 524288 | tf_op jit(solution)/shard_map/all_to_all | solution.py:1121
  9.7 44.4 %collective-permute-start.4 = (s32[2,512]{1,0:T(2,128)}, s32[2,512]{1,0:T(2,128)S(1)}, u32[]{:S(2)}, u32[]{:S(2)}) collective-permute-start(s32[2,512]{1,0:T(2,128)} %param.25), channel_id=1, source_target_pairs={{0,8},{8,0},{1,9},{9,1},{2,10},{10,2},{3,11},{11,3},{4,12},{12,4},... | collective-permute-start | bytes 12296 | tf_op jit(solution)/shard_map/ppermute | solution.py:1037
  45.5 14.7 %all-to-all-start.1 = ((bf16[8,64,256]{2,1,0:T(8,128)(2,1)}), bf16[8,64,256]{2,1,0:T(8,128)(2,1)S(1)}, u32[]{:S(2)}, u32[]{:S(2)}) async-start(bf16[8,64,256]{2,1,0:T(8,128)(2,1)} %bitcast.4), calls=%async_computation.1 | async-start | bytes 524288 | tf_op jit(solution)/shard_map/all_to_all | solution.py:1137
  105.7 35.2 %collective-permute-start.17 = (bf16[2,2,16,768]{3,0,1,2:T(2,128)(2,1)S(1)}, bf16[2,2,16,768]{3,0,1,2:T(2,128)(2,1)S(1)}, u32[]{:S(2)}, u32[]{:S(2)}) collective-permute-start(bf16[2,2,16,768]{3,0,1,2:T(2,128)(2,1)S(1)} %get-tuple-element.411), channel_id=1, source_target_pairs={{0,8},{8,0},{1,9},{9,1},{2,10},{10,2},{3,11},{11,3},{4,12},{12,4},... | collective-permute-start | bytes 294920 | tf_op jit(solution)/shard_map/ppermute | solution.py:1037
  127.8 18.1 %collective-permute-start.14 = (bf16[128,768]{1,0:T(8,128)(2,1)}, bf16[128,768]{1,0:T(8,128)(2,1)}, u32[]{:S(2)}, u32[]{:S(2)}) collective-permute-start(bf16[128,768]{1,0:T(8,128)(2,1)} %get-tuple-element.147.f0), channel_id=1, source_target_pairs={{0,8},{8,0},{1,9},{9,1},{2,10},{10,2},{3,11},{11,3},{4,12},{12,4},... | collective-permute-start | bytes 589832 | tf_op jit(solution)/shard_map/ppermute | solution.py:1037
  141.9 14.8 %all-to-all-start.3 = ((bf16[4,2,16,768]{3,2,1,0:T(8,128)(2,1)}), bf16[4,2,16,768]{3,2,1,0:T(8,128)(2,1)}, u32[]{:S(2)}, u32[]{:S(2)}) async-start(bf16[4,2,16,768]{3,2,1,0:T(8,128)(2,1)} %copy.278), calls=%async_computation.3 | async-start | bytes 393216 | tf_op jit(solution)/shard_map/all_to_all | solution.py:1199
  166.6 21.9 %collective-permute-start.18 = (bf16[128,768]{1,0:T(8,128)(2,1)}, bf16[128,768]{1,0:T(8,128)(2,1)}, u32[]{:S(2)}, u32[]{:S(2)}) collective-permute-start(bf16[128,768]{1,0:T(8,128)(2,1)} %get-tuple-element.154.e0), channel_id=1, source_target_pairs={{0,8},{8,0},{1,9},{9,1},{2,10},{10,2},{3,11},{11,3},{4,12},{12,4},... | collective-permute-start | bytes 589832 | tf_op jit(solution)/shard_map/ppermute | solution.py:1037
  183.8 18.2 %all-to-all-start.2 = ((bf16[4,32,768]{2,1,0:T(8,128)(2,1)}), bf16[4,32,768]{2,1,0:T(8,128)(2,1)}, u32[]{:S(2)}, u32[]{:S(2)}) async-start(bf16[4,32,768]{2,1,0:T(8,128)(2,1)} %copy.275), calls=%async_computation.2 | async-start | bytes 393216 | tf_op jit(solution)/shard_map/all_to_all | solution.py:1189
  203.6 17.4 %collective-permute-start.16 = (bf16[2,32,768]{2,1,0:T(8,128)(2,1)}, bf16[2,32,768]{2,1,0:T(8,128)(2,1)}, u32[]{:S(2)}, u32[]{:S(2)}) collective-permute-start(bf16[2,32,768]{2,1,0:T(8,128)(2,1)} %get-tuple-element.413), channel_id=1, source_target_pairs={{0,8},{8,0},{1,9},{9,1},{2,10},{10,2},{3,11},{11,3},{4,12},{12,4},... | collective-permute-start | bytes 294920 | tf_op jit(solution)/shard_map/ppermute | solution.py:1037
  203.8 19.1 %collective-permute-start.20 = (bf16[128,768]{1,0:T(8,128)(2,1)}, bf16[128,768]{1,0:T(8,128)(2,1)}, u32[]{:S(2)}, u32[]{:S(2)}) collective-permute-start(bf16[128,768]{1,0:T(8,128)(2,1)} %get-tuple-element.161.e0), channel_id=1, source_target_pairs={{0,8},{8,0},{1,9},{9,1},{2,10},{10,2},{3,11},{11,3},{4,12},{12,4},... | collective-permute-start | bytes 589832 | tf_op jit(solution)/shard_map/ppermute | solution.py:1037
  208.3 14.6 %collective-permute-start.22 = (bf16[128,768]{1,0:T(8,128)(2,1)}, bf16[128,768]{1,0:T(8,128)(2,1)}, u32[]{:S(2)}, u32[]{:S(2)}) collective-permute-start(bf16[128,768]{1,0:T(8,128)(2,1)} %collective-permute-done.21.e2), channel_id=1, source_target_pairs={{0,8},{8,0},{1,9},{9,1},{2,10},{10,2},{3,11},{11,3},{4,12},{12,4},... | collective-permute-start | bytes 589832 | tf_op jit(solution)/shard_map/ppermute | solution.py:1037
  216.2 178.1 %collective-permute-start.57 = (bf16[4,2,2,96,768]{4,3,2,1,0:T(8,128)(2,1)}, bf16[4,2,2,96,768]{4,3,2,1,0:T(8,128)(2,1)}, u32[]{:S(2)}, u32[]{:S(2)}) collective-permute-start(bf16[4,2,2,96,768]{4,3,2,1,0:T(8,128)(2,1)} %get-tuple-element.213), channel_id=1, source_target_pairs={{0,16},{16,0},{1,17},{17,1},{2,18},{18,2},{3,19},{19,3},{4,20},{20... | collective-permute-start | bytes 7077896 | tf_op jit(solution)/shard_map/ppermute | solution.py:1037
  242.2 32.1 %collective-permute-start.49 = (bf16[2,2,96,192]{3,1,2,0:T(2,128)(2,1)S(1)}, bf16[2,2,96,192]{3,1,2,0:T(2,128)(2,1)S(1)}, u32[]{:S(2)}, u32[]{:S(2)}) collective-permute-start(bf16[2,2,96,192]{3,1,2,0:T(2,128)(2,1)S(1)} %dynamic-slice_bitcast_fusion.8), channel_id=1, source_target_pairs={{0,16},{16,0},{1,17},{17,1},{2,18},{18,2},{3,19},{19,3},{4,20},{20... | collective-permute-start | bytes 442376 | tf_op jit(solution)/shard_map/ppermute | solution.py:1037
  244.3 45.9 %collective-permute-start.23 = (bf16[2,128,768]{2,1,0:T(8,128)(2,1)}, bf16[2,128,768]{2,1,0:T(8,128)(2,1)}, u32[]{:S(2)}, u32[]{:S(2)}) collective-permute-start(bf16[2,128,768]{2,1,0:T(8,128)(2,1)} %copy-done.95), channel_id=1, source_target_pairs={{0,8},{8,0},{1,9},{9,1},{2,10},{10,2},{3,11},{11,3},{4,12},{12,4},... | collective-permute-start | bytes 1179656 | tf_op jit(solution)/shard_map/ppermute | solution.py:1037
  246.1 47.6 %collective-permute-start.40 = (bf16[2,2,96,640]{3,2,1,0:T(8,128)(2,1)}, bf16[2,2,96,640]{3,2,1,0:T(8,128)(2,1)}, u32[]{:S(2)}, u32[]{:S(2)}) collective-permute-start(bf16[2,2,96,640]{3,2,1,0:T(8,128)(2,1)} %slice.325), channel_id=1, source_target_pairs={{0,2},{2,0},{4,6},{6,4},{1,3},{3,1},{5,7},{7,5},{8,10},{10,8},{12,... | collective-permute-start | bytes 1474568 | tf_op jit(solution)/shard_map/ppermute | solution.py:1042
  295.1 13.7 %collective-permute-start.41 = (bf16[2,96,640]{2,1,0:T(8,128)(2,1)S(1)}, bf16[2,96,640]{2,1,0:T(8,128)(2,1)S(1)}, u32[]{:S(2)}, u32[]{:S(2)}) collective-permute-start(bf16[2,96,640]{2,1,0:T(8,128)(2,1)S(1)} %slice_bitcast_fusion.18), channel_id=1, source_target_pairs={{0,4},{2,6},{4,0},{6,2},{1,5},{3,7},{5,1},{7,3},{8,12},{10,14},{12... | collective-permute-start | bytes 737288 | tf_op jit(solution)/shard_map/ppermute | solution.py:1042
  295.9 69.5 %collective-permute-start.52 = (bf16[96,192]{1,0:T(8,128)(2,1)}, bf16[96,192]{1,0:T(8,128)(2,1)}, u32[]{:S(2)}, u32[]{:S(2)}) collective-permute-start(bf16[96,192]{1,0:T(8,128)(2,1)} %fusion.31), channel_id=1, source_target_pairs={{0,0},{1,4},{2,8},{3,12},{4,1},{5,5},{6,9},{7,13},{8,2},{9,6},{10,... | collective-permute-start | bytes 110600 | tf_op jit(solution)/shard_map/ppermute | solution.py:1288
  347.5 16.6 %collective-permute-start.30 = (bf16[2,128,768]{2,1,0:T(8,128)(2,1)S(1)}, bf16[2,128,768]{2,1,0:T(8,128)(2,1)S(1)}, u32[]{:S(2)}, u32[]{:S(2)}) collective-permute-start(bf16[2,128,768]{2,1,0:T(8,128)(2,1)S(1)} %get-tuple-element.186), channel_id=1, source_target_pairs={{0,8},{8,0},{1,9},{9,1},{2,10},{10,2},{3,11},{11,3},{4,12},{12,4},... | collective-permute-start | bytes 1179656 | tf_op jit(solution)/shard_map/ppermute | solution.py:1037
  348.4 16.0 %collective-permute-start.35 = (bf16[2,2,96,640]{3,2,1,0:T(8,128)(2,1)}, bf16[2,2,96,640]{3,2,1,0:T(8,128)(2,1)S(1)}, u32[]{:S(2)}, u32[]{:S(2)}) collective-permute-start(bf16[2,2,96,640]{3,2,1,0:T(8,128)(2,1)} %slice.309), channel_id=1, source_target_pairs={{0,2},{2,0},{4,6},{6,4},{1,3},{3,1},{5,7},{7,5},{8,10},{10,8},{12,... | collective-permute-start | bytes 1474568 | tf_op jit(solution)/shard_map/ppermute | solution.py:1042
  362.8 109.0 %collective-permute-start.53 = (bf16[4,2,2,96,768]{4,3,2,1,0:T(8,128)(2,1)}, bf16[4,2,2,96,768]{4,3,2,1,0:T(8,128)(2,1)}, u32[]{:S(2)}, u32[]{:S(2)}) collective-permute-start(bf16[4,2,2,96,768]{4,3,2,1,0:T(8,128)(2,1)} %get-tuple-element.209), channel_id=1, source_target_pairs={{0,16},{16,0},{1,17},{17,1},{2,18},{18,2},{3,19},{19,3},{4,20},{20... | collective-permute-start | bytes 7077896 | tf_op jit(solution)/shard_map/ppermute | solution.py:1037
  364.1 68.7 %collective-permute-start.44 = (bf16[96,192]{0,1:T(8,128)(2,1)}, bf16[96,192]{0,1:T(8,128)(2,1)S(1)}, u32[]{:S(2)}, u32[]{:S(2)}) collective-permute-start(bf16[96,192]{0,1:T(8,128)(2,1)} %get-tuple-element.424), channel_id=1, source_target_pairs={{0,8},{8,0},{1,9},{9,1},{2,10},{10,2},{3,11},{11,3},{4,12},{12,4},... | collective-permute-start | bytes 110600 | tf_op jit(solution)/shard_map/ppermute | solution.py:1037
  392.7 26.3 %collective-permute-start.38 = (bf16[3,96,192]{1,2,0:T(8,128)(2,1)S(1)}, bf16[3,96,192]{1,2,0:T(8,128)(2,1)S(1)}, u32[]{:S(2)}, u32[]{:S(2)}) collective-permute-start(bf16[3,96,192]{1,2,0:T(8,128)(2,1)S(1)} %broadcast_select_fusion.5), channel_id=1, source_target_pairs={{0,16},{16,0},{1,17},{17,1},{2,18},{18,2},{3,19},{19,3},{4,20},{20... | collective-permute-start | bytes 331784 | tf_op jit(solution)/shard_map/ppermute | solution.py:1037
  399.3 64.2 %collective-permute-start.58 = (bf16[2,2,2,96,768]{4,3,2,1,0:T(8,128)(2,1)}, bf16[2,2,2,96,768]{4,3,2,1,0:T(8,128)(2,1)}, u32[]{:S(2)}, u32[]{:S(2)}) collective-permute-start(bf16[2,2,2,96,768]{4,3,2,1,0:T(8,128)(2,1)} %slice.355), channel_id=1, source_target_pairs={{0,2},{2,0},{4,6},{6,4},{1,3},{3,1},{5,7},{7,5},{8,10},{10,8},{12,... | collective-permute-start | bytes 3538952 | tf_op jit(solution)/shard_map/ppermute | solution.py:1042
  401.3 31.4 %all-to-all-start.4 = ((bf16[8,64,256]{2,1,0:T(8,128)(2,1)}), bf16[8,64,256]{2,1,0:T(8,128)(2,1)S(1)}, u32[]{:S(2)}, u32[]{:S(2)}) async-start(bf16[8,64,256]{2,1,0:T(8,128)(2,1)} %get-tuple-element.191), calls=%async_computation.4 | async-start | bytes 524288 | tf_op jit(solution)/shard_map/all_to_all | solution.py:1297
  419.2 13.6 %collective-permute-start.39 = (bf16[96,192]{0,1:T(8,128)(2,1)S(1)}, bf16[96,192]{0,1:T(8,128)(2,1)S(1)}, u32[]{:S(2)}, u32[]{:S(2)}) collective-permute-start(bf16[96,192]{0,1:T(8,128)(2,1)S(1)} %get-tuple-element.415), channel_id=1, source_target_pairs={{0,8},{8,0},{1,9},{9,1},{2,10},{10,2},{3,11},{11,3},{4,12},{12,4},... | collective-permute-start | bytes 110600 | tf_op jit(solution)/shard_map/ppermute | solution.py:1037
  447.9 27.4 %collective-permute-start.33 = (bf16[2,1536,128]{2,1,0:T(8,128)(2,1)}, bf16[2,1536,128]{2,1,0:T(8,128)(2,1)}, u32[]{:S(2)}, u32[]{:S(2)}) collective-permute-start(bf16[2,1536,128]{2,1,0:T(8,128)(2,1)} %get-tuple-element.197), channel_id=1, source_target_pairs={{0,8},{8,0},{1,9},{9,1},{2,10},{10,2},{3,11},{11,3},{4,12},{12,4},... | collective-permute-start | bytes 2359304 | tf_op jit(solution)/shard_map/ppermute | solution.py:1037
  447.9 13.4 %collective-permute-start.62 = (f32[27,96]{1,0:T(8,128)S(1)}, f32[27,96]{1,0:T(8,128)S(1)}, u32[]{:S(2)}, u32[]{:S(2)}) collective-permute-start(f32[27,96]{1,0:T(8,128)S(1)} %add.376), channel_id=1, source_target_pairs={{0,16},{16,0},{1,17},{17,1},{2,18},{18,2},{3,19},{19,3},{4,20},{20... | collective-permute-start | bytes 31112 | tf_op jit(solution)/shard_map/ppermute | solution.py:1037
  466.8 29.5 %collective-permute-start.59 = (bf16[2,2,96,768]{3,2,1,0:T(8,128)(2,1)}, bf16[2,2,96,768]{3,2,1,0:T(8,128)(2,1)}, u32[]{:S(2)}, u32[]{:S(2)}) collective-permute-start(bf16[2,2,96,768]{3,2,1,0:T(8,128)(2,1)} %slice_bitcast_fusion.8), channel_id=1, source_target_pairs={{0,4},{2,6},{4,0},{6,2},{1,5},{3,7},{5,1},{7,3},{8,12},{10,14},{12... | collective-permute-start | bytes 1769480 | tf_op jit(solution)/shard_map/ppermute | solution.py:1042
  474.2 38.3 %collective-permute-start.54 = (bf16[2,2,2,96,768]{4,3,2,1,0:T(8,128)(2,1)S(1)}, bf16[2,2,2,96,768]{4,3,2,1,0:T(8,128)(2,1)S(1)}, u32[]{:S(2)}, u32[]{:S(2)}) collective-permute-start(bf16[2,2,2,96,768]{4,3,2,1,0:T(8,128)(2,1)S(1)} %slice.349), channel_id=1, source_target_pairs={{0,2},{2,0},{4,6},{6,4},{1,3},{3,1},{5,7},{7,5},{8,10},{10,8},{12,... | collective-permute-start | bytes 3538952 | tf_op jit(solution)/shard_map/ppermute | solution.py:1042
  476.8 41.7 %collective-permute-start.34 = (bf16[1536,128]{1,0:T(8,128)(2,1)S(1)}, bf16[1536,128]{1,0:T(8,128)(2,1)S(1)}, u32[]{:S(2)}, u32[]{:S(2)}) collective-permute-start(bf16[1536,128]{1,0:T(8,128)(2,1)S(1)} %get-tuple-element.402), channel_id=1, source_target_pairs={{0,16},{16,0},{1,17},{17,1},{2,18},{18,2},{3,19},{19,3},{4,20},{20... | collective-permute-start | bytes 1179656 | tf_op jit(solution)/shard_map/ppermute | solution.py:1037
  514.7 27.0 %collective-permute-start.55 = (bf16[2,2,96,768]{3,2,1,0:T(8,128)(2,1)}, bf16[2,2,96,768]{3,2,1,0:T(8,128)(2,1)}, u32[]{:S(2)}, u32[]{:S(2)}) collective-permute-start(bf16[2,2,96,768]{3,2,1,0:T(8,128)(2,1)} %slice_bitcast_fusion.10), channel_id=1, source_target_pairs={{0,4},{2,6},{4,0},{6,2},{1,5},{3,7},{5,1},{7,3},{8,12},{10,14},{12... | collective-permute-start | bytes 1769480 | tf_op jit(solution)/shard_map/ppermute | solution.py:1042
  516.6 29.6 %collective-permute-start.60 = (bf16[2,96,768]{2,1,0:T(8,128)(2,1)}, bf16[2,96,768]{2,1,0:T(8,128)(2,1)S(1)}, u32[]{:S(2)}, u32[]{:S(2)}) collective-permute-start(bf16[2,96,768]{2,1,0:T(8,128)(2,1)} %slice_bitcast_fusion.14), channel_id=1, source_target_pairs={{0,1},{1,0},{2,3},{3,2},{4,5},{5,4},{6,7},{7,6},{8,9},{9,8},{10,11... | collective-permute-start | bytes 884744 | tf_op jit(solution)/shard_map/ppermute | solution.py:1037
  (223 other events, 1479.8 us)
